TPU v7x, 128 devices: a whole 4x4x4 slice. The times are simulated.
128 devices in a mesh: dp: 16 (over z, x), mp: 8 (over y, core).
Axes of the slice: x: 4, y: 4, z: 4, core: 2. Of those that a mesh axis runs over, the one named last changes fastest.
Arguments:
- queries: bfloat16 [8192, 8192], P('dp', 'mp'), may hold values from -160 to 160
- out_grad: bfloat16 [8192, 8192], P('dp', 'mp'), may hold values from -6 to 6
- response_keys: bfloat16 [8192, 1024], P('dp', 'mp'), may hold values from -6 to 6
- response_values: bfloat16 [8192, 1024], P('dp', 'mp'), may hold values from -6 to 6
- prefix_keys: bfloat16 [16384, 1024], P('dp', 'mp'), may hold values from -48 to 48
- prefix_values: bfloat16 [16384, 1024], P('dp', 'mp'), may hold values from -6 to 6
- q_weight: bfloat16 [8192, 8192], P(None, 'mp'), may hold values from -0.0625 to 0.0625
- block_prompt: int32 [32], P('dp'), may hold values from 0 to 15, as said below
- response_lengths: int32 [32, 4], P('dp'), may hold values from 1 to 128, 256 in all within a row
Outputs:
- input_grad: bfloat16 [8192, 8192], P('dp', 'mp')
- response_key_grad: bfloat16 [8192, 1024], P('dp', 'mp')
- response_value_grad: bfloat16 [8192, 1024], P('dp', 'mp')
- prefix_key_grad: bfloat16 [16384, 1024], P('dp', 'mp')
- prefix_value_grad: bfloat16 [16384, 1024], P('dp', 'mp')
Inputs may be any that keep to these rules, and one draw needn't show every extreme that they name: `block_prompt`: every prompt is answered by at least one block; some prompts by several.
All inputs are finite; a program needn't handle non-finite values.
Results may differ from a plain program's by a relative error of at most 0.017.
Values may be sent and summed in bfloat16 or wider, within the bound.
A program may use at most 192 MiB of HBM per device.

v0:
```python
import jax
import jax.numpy as jnp
from jax import lax
from jax.sharding import PartitionSpec as P

HEAD_DIM = 128


def segment_rows(lengths, block):
    ends = jnp.cumsum(lengths, axis=-1)
    places = jnp.arange(block, dtype=jnp.int32)
    return jnp.sum((places[:, None] >= ends[None, :]).astype(jnp.int32), axis=1)


def block_grads(query, pre_k, pre_v, own_k, own_v, d_out, seg):
    f32 = jnp.float32
    rows = query.shape[0]
    kvn = own_k.shape[1] // HEAD_DIM
    group = query.shape[1] // HEAD_DIM // kvn
    scale = HEAD_DIM ** (-0.5)
    quer = query.reshape(rows, kvn, group, HEAD_DIM)
    dout = d_out.reshape(rows, kvn, group, HEAD_DIM)
    keys = jnp.concatenate([pre_k, own_k], 0).reshape(-1, kvn, HEAD_DIM)
    vals = jnp.concatenate([pre_v, own_v], 0).reshape(-1, kvn, HEAD_DIM)
    score = jnp.einsum("rkgd,skd->kgrs", quer, keys, preferred_element_type=f32) * scale
    places = jnp.arange(rows, dtype=jnp.int32)
    own = (seg[None, :] == seg[:, None]) & (places[None, :] <= places[:, None])
    mask = jnp.concatenate([jnp.ones((rows, pre_k.shape[0]), bool), own], 1)
    score = jnp.where(mask, score, -1e30)
    top = jnp.max(score, axis=-1, keepdims=True)
    expo = jnp.exp(score - top)
    prob = expo / jnp.sum(expo, axis=-1, keepdims=True)
    prob_low = prob.astype(jnp.bfloat16)
    output = jnp.einsum("kgrs,skd->rkgd", prob_low, vals, preferred_element_type=f32)
    delta = jnp.sum(dout.astype(f32) * output, axis=-1)
    dprob = jnp.einsum("rkgd,skd->kgrs", dout, vals, preferred_element_type=f32)
    dscore = prob * (dprob - jnp.transpose(delta, (1, 2, 0))[..., None])
    dscore_low = dscore.astype(jnp.bfloat16)
    query_grad = (
        (jnp.einsum("kgrs,skd->rkgd", dscore_low, keys, preferred_element_type=f32) * scale)
        .reshape(rows, -1)
        .astype(jnp.bfloat16)
    )
    key_grad = (
        jnp.einsum("kgrs,rkgd->skd", dscore_low, quer, preferred_element_type=f32) * scale
    ).reshape(-1, kvn * HEAD_DIM)
    value_grad = jnp.einsum("kgrs,rkgd->skd", prob_low, dout, preferred_element_type=f32).reshape(
        -1, kvn * HEAD_DIM
    )
    prefix = pre_k.shape[0]
    return (
        query_grad,
        key_grad[:prefix],
        value_grad[:prefix],
        key_grad[prefix:],
        value_grad[prefix:],
    )


def shards(
    queries,
    out_grad,
    response_keys,
    response_values,
    prefix_keys,
    prefix_values,
    q_weight,
    block_prompt,
    response_lengths,
):
    owners = lax.axis_size("dp")
    prefix = prefix_keys.shape[0]
    width = prefix_keys.shape[1]
    count = block_prompt.shape[0]
    block = queries.shape[0] // count
    all_keys, all_values = (
        lax.all_gather(prefix_keys, "dp", axis=0, tiled=True),
        lax.all_gather(prefix_values, "dp", axis=0, tiled=True),
    )
    query_parts = []
    own_k_parts = []
    own_v_parts = []
    table_k = jnp.zeros((owners * prefix, width), jnp.float32)
    table_v = jnp.zeros((owners * prefix, width), jnp.float32)
    for index in range(count):
        start = block_prompt[index] * prefix
        lower = index * block
        upper = lower + block
        pre_k = lax.dynamic_slice_in_dim(all_keys, start, prefix, 0)
        pre_v = lax.dynamic_slice_in_dim(all_values, start, prefix, 0)
        seg = segment_rows(response_lengths[index], block)
        query_grad, pre_dk, pre_dv, own_dk, own_dv = block_grads(
            queries[lower:upper],
            pre_k,
            pre_v,
            response_keys[lower:upper],
            response_values[lower:upper],
            out_grad[lower:upper],
            seg,
        )
        query_parts.append(query_grad)
        own_k_parts.append(own_dk.astype(jnp.bfloat16))
        own_v_parts.append(own_dv.astype(jnp.bfloat16))
        table_k = lax.dynamic_update_slice_in_dim(
            table_k, lax.dynamic_slice_in_dim(table_k, start, prefix, 0) + pre_dk, start, 0
        )
        table_v = lax.dynamic_update_slice_in_dim(
            table_v, lax.dynamic_slice_in_dim(table_v, start, prefix, 0) + pre_dv, start, 0
        )
    summed_k, summed_v = (
        lax.psum_scatter(
            table_k.astype(jnp.bfloat16), "dp", scatter_dimension=0, tiled=True
        ).astype(jnp.float32),
        lax.psum_scatter(
            table_v.astype(jnp.bfloat16), "dp", scatter_dimension=0, tiled=True
        ).astype(jnp.float32),
    )
    flat_grad = jnp.concatenate(query_parts, 0)
    summed = lax.psum_scatter(
        lax.dot_general(
            q_weight, flat_grad, (((1,), (1,)), ((), ())), preferred_element_type=jnp.float32
        ).astype(jnp.bfloat16),
        "mp",
        scatter_dimension=0,
        tiled=True,
    ).astype(jnp.float32)
    input_grad = summed.T.astype(jnp.bfloat16)
    return (
        input_grad,
        jnp.concatenate(own_k_parts, 0),
        jnp.concatenate(own_v_parts, 0),
        summed_k.astype(jnp.bfloat16),
        summed_v.astype(jnp.bfloat16),
    )


def solution(mesh):
    return jax.shard_map(
        shards,
        mesh=mesh,
        in_specs=(
            P("dp", "mp"),
            P("dp", "mp"),
            P("dp", "mp"),
            P("dp", "mp"),
            P("dp", "mp"),
            P("dp", "mp"),
            P(None, "mp"),
            P("dp"),
            P("dp", None),
        ),
        out_specs=(P("dp", "mp"), P("dp", "mp"), P("dp", "mp"), P("dp", "mp"), P("dp", "mp")),
        check_vma=False,
    )
```

profile of v0, /device:TPU:1, one launch (start us, length us, event | category | flops | bytes accessed | tf_op | source)
XLA Modules:
  0.0 341.5 jit_solution(17597673184381415951)
XLA Ops:
  17.5 47.6 %all-gather.3.cloned.1.call-done = bf16[16384,128]{1,0:T(8,128)(2,1)} async-done(((bf16[1024,128]{1,0:T(8,128)(2,1)}), bf16[16384,128]{1,0:T(8,128)(2,1)}) %all-gather.3.cloned.1.call-update) | async-done | bytes 4194320 | tf_op jit(solution)/shard_map/all_gather | solution.py:77
  66.1 1.7 fusion.9
  67.9 2.2 fusion.6
  70.0 2.8 fusion.29
  73.7 1.7 fusion.10
  75.4 2.2 fusion.8
  77.6 2.8 fusion.41
  81.2 2.3 convert_element_type.133
  83.6 1.7 fusion.116
  85.2 33.2 %all-gather.5.cloned.1.call-done = bf16[16384,128]{1,0:T(8,128)(2,1)} async-done(((bf16[1024,128]{1,0:T(8,128)(2,1)}), bf16[16384,128]{1,0:T(8,128)(2,1)}) %all-gather.5.cloned.1.call-update) | async-done | bytes 4194320 | tf_op jit(solution)/shard_map/all_gather | solution.py:78
  118.5 1.8 constant_dynamic-slice_fusion.2
  120.3 7.2 %fusion.77 = f32[256,8]{0,1:T(8,128)S(1)} fusion(bf16[256,1,8,128]{0,3,2,1:T(8,128)(2,1)} %bitcast.282, bf16[256,128]{1,0:T(8,128)(2,1)} %get-tuple-element.15, bf16[1024,128]{1,0:T(8,128)(2,1)S(1)} %get-tuple-element.7, f32[8,256]{1,0:T(8,128)} %copy-done.22, f32[8,256]{1,0:T(8,128)S(1)} %get-tuple-element.23, f32[1280,256,8]{1,0,2:T(8,128)} %copy-done.1, ...), kind=kOutput, calls=%fused_computation.52 | convolution fusion | flops 685635584 | bytes 11689984 | tf_op jit(solution)/shard_map/kgrs,skd->rkgd/dot_general | solution.py:34
  127.6 5.8 %fusion.4 = bf16[1,8,256,1280]{2,3,1,0:T(8,128)(2,1)} fusion(bf16[256,8,128]{0,2,1:T(8,128)(2,1)S(1)} %bitcast.283, f32[8,256]{1,0:T(8,128)S(1)} %bitcast.287, f32[8,256]{1,0:T(8,128)S(1)} %copy-done.23, f32[8,256]{1,0:T(8,128)S(1)} %get-tuple-element.23, f32[1280,256,8]{1,0,2:T(8,128)S(1)} %bitcast.271, pred[256,1280]{0,1:T(8,128)(4,1)S(1)} %concatenate.28, ...), kind=kOutput, calls=%fused_computation.8 | convolution fusion | flops 690094080 | bytes 16932864 | tf_op jit(solution)/shard_map/rkgd,skd->kgrs/dot_general | solution.py:36
  133.4 4.1 %fusion.38 = f32[1280,1,128]{2,0,1:T(8,128)S(1)} fusion(bf16[256,8,128]{0,2,1:T(8,128)(2,1)S(1)} %bitcast.275, bf16[1,8,256,1280]{2,3,1,0:T(8,128)(2,1)} %fusion.4), kind=kOutput, calls=%fused_computation.39 | convolution fusion | flops 671252480 | bytes 6422528 | tf_op jit(solution)/shard_map/kgrs,rkgd->skd/dot_general | solution.py:45
  138.2 3.0 fusion.80
  141.2 4.1 %fusion.2 = bf16[1,8,256,1280]{2,3,1,0:T(8,128)(2,1)S(1)} fusion(bf16[256,8,128]{0,2,1:T(8,128)(2,1)S(1)} %bitcast.280, f32[8,256]{1,0:T(8,128)S(1)} %bitcast.288, f32[8,256]{1,0:T(8,128)S(1)} %copy-done.21, f32[8,256]{1,0:T(8,128)S(1)} %get-tuple-element.21, f32[1280,256,8]{1,0,2:T(8,128)S(1)} %bitcast.269, pred[256,1280]{0,1:T(8,128)(4,1)S(1)} %concatenate.31, ...), kind=kOutput, calls=%fused_computation.4 | convolution fusion | flops 690094080 | bytes 16932864 | tf_op jit(solution)/shard_map/rkgd,skd->kgrs/dot_general | solution.py:36
  145.3 1.5 fusion.50
  147.6 2.2 convert_element_type.132
  149.9 3.5 %fusion.71 = bf16[128,8,256]{2,0,1:T(8,128)(2,1)S(1)} fusion(bf16[1,8,256,1280]{2,3,1,0:T(8,128)(2,1)} %copy-done.2, bf16[256,128]{1,0:T(8,128)(2,1)S(1)} %copy-done.10, bf16[1024,128]{1,0:T(8,128)(2,1)S(1)} %copy-done.6), kind=kOutput, calls=%fused_computation.50 | convolution fusion | flops 672268288 | bytes 6094848 | tf_op jit(solution)/shard_map/kgrs,skd->rkgd/dot_general | solution.py:40
  153.4 3.4 %fusion.74 = bf16[128,8,256]{2,0,1:T(8,128)(2,1)S(1)} fusion(bf16[1,8,256,1280]{2,3,1,0:T(8,128)(2,1)} %fusion.4, bf16[256,128]{1,0:T(8,128)(2,1)S(1)} %copy-done.8, bf16[1024,128]{1,0:T(8,128)(2,1)S(1)} %get-tuple-element.5), kind=kOutput, calls=%fused_computation.51 | convolution fusion | flops 672268288 | bytes 6094848 | tf_op jit(solution)/shard_map/kgrs,skd->rkgd/dot_general | solution.py:40
  156.9 30.6 %fusion = bf16[8192,512]{0,1:T(8,128)(2,1)} fusion(bf16[8192,1024]{1,0:T(8,128)(2,1)} %param.15, bf16[256,1024]{0,1:T(8,128)(2,1)S(1)} %bitcast.276, bf16[256,1024]{0,1:T(8,128)(2,1)S(1)} %bitcast.277), kind=kOutput, calls=%fused_computation.1 | convolution fusion | flops 8596226048 | bytes 26214400 | tf_op jit(solution)/shard_map/dot_general | solution.py:120
  189.8 8.3 %reduce-scatter.8.cloned.1.call-done = bf16[1024,128]{1,0:T(8,128)(2,1)} async-done(((bf16[16384,128]{1,0:T(8,128)(2,1)}), bf16[1024,128]{1,0:T(8,128)(2,1)}) %reduce-scatter.8.cloned.1.call-update) | async-done | bytes 262160 | tf_op jit(solution)/shard_map/reduce_scatter | solution.py:114
  198.1 81.2 %reduce-scatter.6.cloned.1.call-done = bf16[1024,128]{1,0:T(8,128)(2,1)} async-done(((bf16[16384,128]{1,0:T(8,128)(2,1)}), bf16[1024,128]{1,0:T(8,128)(2,1)}) %reduce-scatter.6.cloned.1.call-update) | async-done | bytes 262160 | tf_op jit(solution)/shard_map/reduce_scatter | solution.py:111
  279.3 55.6 %reduce-scatter.4.cloned.1.call-done = bf16[1024,512]{0,1:T(8,128)(2,1)} async-done(((bf16[8192,512]{0,1:T(8,128)(2,1)}), bf16[1024,512]{0,1:T(8,128)(2,1)}) %reduce-scatter.4.cloned.1.call-update) | async-done | bytes 1048592 | tf_op jit(solution)/shard_map/reduce_scatter | solution.py:119
  (100 shorter events, 15.5 us)
Async XLA Ops:
  7.2 57.9 %all-gather.3.cloned.1.call-start = ((), (), s32[]{:S(2)}) async-start(), calls=%async_computation.3 | async-start | bytes 4456448 | tf_op jit(solution)/shard_map/all_gather | solution.py:77
  7.9 110.6 %all-gather.5.cloned.1.call-start = ((), (), s32[]{:S(2)}) async-start(), calls=%async_computation.4 | async-start | bytes 4456448 | tf_op jit(solution)/shard_map/all_gather | solution.py:78
  8.6 189.5 %reduce-scatter.8.cloned.1.call-start = ((), (), s32[]{:S(2)}) async-start(), calls=%async_computation.7 | async-start | bytes 4456448 | tf_op jit(solution)/shard_map/reduce_scatter | solution.py:114
  14.5 53.4 %copy-start.3 = (bf16[256,1024]{0,1:T(8,128)(2,1)}, bf16[256,1024]{0,1:T(8,128)(2,1)S(1)}, u32[]{:S(2)}) copy-start(bf16[256,1024]{0,1:T(8,128)(2,1)S(1)} %copy.84) | copy-start | bytes 1572868
  16.2 53.9 %copy-start.15 = (bf16[256,1024]{0,1:T(8,128)(2,1)}, bf16[256,1024]{0,1:T(8,128)(2,1)S(1)}, u32[]{:S(2)}) copy-start(bf16[256,1024]{0,1:T(8,128)(2,1)S(1)} %copy.85) | copy-start | bytes 1572868
  16.4 61.2 %copy-start.13 = (bf16[256,1024]{0,1:T(8,128)(2,1)}, bf16[256,1024]{0,1:T(8,128)(2,1)S(1)}, u32[]{:S(2)}) copy-start(bf16[256,1024]{0,1:T(8,128)(2,1)S(1)} %copy.87) | copy-start | bytes 1572868
  17.5 50.4 %copy-start.7 = (bf16[256,128]{1,0:T(8,128)(2,1)}, bf16[256,128]{1,0:T(8,128)(2,1)S(1)}, u32[]{:S(2)}) copy-start(bf16[256,128]{1,0:T(8,128)(2,1)S(1)} %get-tuple-element.13) | copy-start | bytes 196612
  17.5 56.2 %copy-start.9 = (bf16[256,128]{1,0:T(8,128)(2,1)}, bf16[256,128]{1,0:T(8,128)(2,1)S(1)}, u32[]{:S(2)}) copy-start(bf16[256,128]{1,0:T(8,128)(2,1)S(1)} %get-tuple-element.14) | copy-start | bytes 196612
  66.1 7.6 %copy-start.5 = (bf16[1024,128]{1,0:T(8,128)(2,1)}, bf16[1024,128]{1,0:T(8,128)(2,1)S(1)}, u32[]{:S(2)}) copy-start(bf16[1024,128]{1,0:T(8,128)(2,1)S(1)} %get-tuple-element.6) | copy-start | bytes 786436
  67.8 5.0 %copy-start.1 = (f32[1280,256,8]{1,0,2:T(8,128)}, f32[1280,256,8]{1,0,2:T(8,128)S(1)}, u32[]{:S(2)}) copy-start(f32[1280,256,8]{1,0,2:T(8,128)S(1)} %get-tuple-element.24) | copy-start | bytes 31457284
  75.4 5.0 %copy-start = (f32[1280,256,8]{1,0,2:T(8,128)}, f32[1280,256,8]{1,0,2:T(8,128)S(1)}, u32[]{:S(2)}) copy-start(f32[1280,256,8]{1,0,2:T(8,128)S(1)} %get-tuple-element.22) | copy-start | bytes 31457284
  83.5 44.0 %slice-start.3 = ((s8[10485760]{0:T(1024)(128)(4,1)}), s8[2097152]{0:T(1024)(128)(4,1)S(1)}, s32[]{:S(2)}) async-start(s8[10485760]{0:T(1024)(128)(4,1)} %bitcast.270), calls=%async_computation.11 | async-start | bytes 4194304
  83.5 195.8 %reduce-scatter.6.cloned.1.call-start = ((), (), s32[]{:S(2)}) async-start(), calls=%async_computation.6 | async-start | bytes 4456448 | tf_op jit(solution)/shard_map/reduce_scatter | solution.py:111
  120.2 7.3 %slice-start.4 = ((s8[10485760]{0:T(1024)(128)(4,1)}), s8[4194304]{0:T(1024)(128)(4,1)S(1)}, s32[]{:S(2)}) async-start(s8[10485760]{0:T(1024)(128)(4,1)} %bitcast.270), calls=%async_computation.12 | async-start | bytes 8388608
  120.2 7.3 %slice-start.5 = ((s8[10485760]{0:T(1024)(128)(4,1)}), s8[4194304]{0:T(1024)(128)(4,1)S(1)}, s32[]{:S(2)}) async-start(s8[10485760]{0:T(1024)(128)(4,1)} %bitcast.270), calls=%async_computation.13 | async-start | bytes 8388608
  120.2 7.3 %copy-start.16 = (bf16[256,1024]{0,1:T(8,128)(2,1)S(1)}, bf16[256,1024]{0,1:T(8,128)(2,1)}, u32[]{:S(2)}) copy-start(bf16[256,1024]{0,1:T(8,128)(2,1)} %copy-done.15) | copy-start | bytes 1572868
  120.2 7.3 %copy-start.19 = (bf16[256,128]{1,0:T(8,128)(2,1)S(1)}, bf16[256,128]{1,0:T(8,128)(2,1)}, u32[]{:S(2)}) copy-start(bf16[256,128]{1,0:T(8,128)(2,1)} %get-tuple-element.15) | copy-start | bytes 196612
  120.2 7.3 %copy-start.23 = (f32[8,256]{1,0:T(8,128)S(1)}, f32[8,256]{1,0:T(8,128)}, u32[]{:S(2)}) copy-start(f32[8,256]{1,0:T(8,128)} %copy-done.22) | copy-start | bytes 24580
  120.3 17.9 %slice-start = ((s8[10485760]{0:T(1024)(128)(4,1)}), s8[4194304]{0:T(1024)(128)(4,1)S(1)}, s32[]{:S(2)}) async-start(s8[10485760]{0:T(1024)(128)(4,1)} %bitcast.268), calls=%async_computation.8 | async-start | bytes 8388608
  120.3 17.9 %slice-start.1 = ((s8[10485760]{0:T(1024)(128)(4,1)}), s8[4194304]{0:T(1024)(128)(4,1)S(1)}, s32[]{:S(2)}) async-start(s8[10485760]{0:T(1024)(128)(4,1)} %bitcast.268), calls=%async_computation.9 | async-start | bytes 8388608
  127.6 5.8 %copy-start.4 = (bf16[256,1024]{0,1:T(8,128)(2,1)S(1)}, bf16[256,1024]{0,1:T(8,128)(2,1)}, u32[]{:S(2)}) copy-start(bf16[256,1024]{0,1:T(8,128)(2,1)} %copy-done.3) | copy-start | bytes 1572868
  127.6 10.5 %slice-start.2 = ((s8[10485760]{0:T(1024)(128)(4,1)}), s8[2097152]{0:T(1024)(128)(4,1)S(1)}, s32[]{:S(2)}) async-start(s8[10485760]{0:T(1024)(128)(4,1)} %bitcast.268), calls=%async_computation.10 | async-start | bytes 4194304
  147.6 5.8 %copy-start.8 = (bf16[256,128]{1,0:T(8,128)(2,1)S(1)}, bf16[256,128]{1,0:T(8,128)(2,1)}, u32[]{:S(2)}) copy-start(bf16[256,128]{1,0:T(8,128)(2,1)} %copy-done.7) | copy-start | bytes 196612
  149.9 185.1 %reduce-scatter.4.cloned.1.call-start = ((), (), s32[]{:S(2)}) async-start(), calls=%async_computation.5 | async-start | bytes 9437184 | tf_op jit(solution)/shard_map/reduce_scatter | solution.py:119
  (11 other events, 36.7 us)
Sparse Core Ops, SparseCore 0:
  10.1 54.8 all-gather.2
  67.2 51.2 all-gather.4
  122.4 75.6 reduce-scatter.7
  202.2 77.0 reduce-scatter.5
  282.1 52.7 reduce-scatter.3
where the time goes:
time: 342 us; the launch traced here: 341 us
  waiting for transfers between devices  227 us (66%)
  matrix products  72.1 us (21%)
  between operations  15.7 us (5%)
  local copies, waits for them, and re-layouts  15.1 us (4%)
  other arithmetic  11 us (3%)
    reduce_scatter x1, waiting for transfers between devices, shards(): lax.psum_scatter(table_k.astype(jnp.bfloat16), 'dp', scatter_dimension=0,...  81.2 us
    reduce_scatter x1, waiting for transfers between devices, shards(): lax.psum_scatter(lax.dot_general(q_weight, flat_grad, (((1,), (1,)), ((),...  55.6 us
    all_gather x1, waiting for transfers between devices, shards(): lax.all_gather(prefix_keys, 'dp', axis=0, tiled=True)  47.6 us
    all_gather x1, waiting for transfers between devices, shards(): lax.all_gather(prefix_values, 'dp', axis=0, tiled=True)  33.2 us
    dot_general x1, matrix products, shards(): lax.dot_general(q_weight, flat_grad, (((1,), (1,)), ((), ())), preferred_...  30.6 us
    dot_general x2, matrix products, block_grads(): jnp.einsum('kgrs,skd->rkgd', prob_low, vals, preferred_element_type=f32)  10.2 us
    dot_general x2, matrix products, block_grads(): dprob = jnp.einsum('rkgd,skd->kgrs', dout, vals, preferred_element_type=f32)  9.84 us
    reduce_scatter x1, waiting for transfers between devices, shards(): lax.psum_scatter(table_v.astype(jnp.bfloat16), 'dp', scatter_dimension=0,...  8.31 us
  transfers between devices with their start and end apart: 5, of which 5 were waited for; matrix products, arithmetic and copies ran while one was open for 28% of the time, Pallas kernels for 0%

commit v1 on v0

v1 whole, which is shorter than its diff:
```python
import functools

import jax
import jax.numpy as jnp
from jax import lax
from jax.experimental import pallas as pl
from jax.experimental.pallas import tpu as pltpu
from jax.sharding import PartitionSpec as P

HEAD_DIM = 128
GROUP = 16
SCALE = HEAD_DIM ** (-0.5)
LOG2E = 1.4426950408889634
MESH = pl.DeviceIdType.MESH
F32 = jnp.float32
BF16 = jnp.bfloat16


def dot(a, b):
    return jnp.dot(a, b, preferred_element_type=F32)


def dot_nt(a, b):
    return lax.dot_general(a, b, (((1,), (1,)), ((), ())), preferred_element_type=F32)


def fold(x, op):
    rows, cols = x.shape
    return op(x.reshape(rows // 8, 8, cols), axis=0)


def kernel(
    n,
    nmp,
    prompt_ref,
    lengths_ref,
    q_hbm,
    do_hbm,
    rk_hbm,
    rv_hbm,
    pk_hbm,
    pv_hbm,
    w_hbm,
    out_hbm,
    own_hbm,
    pre_hbm,
    q_v,
    do_v,
    own_v,
    w_v,
    tile_v,
    table_v,
    spread_v,
    choose_v,
    send_v,
    pre_v,
    keys_t,
    score_v,
    dprob_v,
    grad_v,
    qg_v,
    ownout_v,
    back_v,
    gather_v,
    home_v,
    part_v,
    sib_v,
    opp_v,
    hop_v,
    near_v,
    side_v,
    sum_v,
    in_sem,
    w_sem,
    s1_send,
    s1_recv,
    t_send,
    t_recv,
    s2_send,
    s2_recv,
    b_send,
    b_recv,
    h_send,
    h_recv,
    sib_send,
    sib_recv,
    opp_send,
    opp_recv,
    raw_send,
    raw_recv,
    mix_send,
    mix_recv,
    out_sem,
):
    me = lax.axis_index("dp")
    mp = lax.axis_index("mp")
    ny = nmp // 2
    y, core = mp // 2, lax.rem(mp, 2)
    y_right, y_left, y_opp = lax.rem(y + 1, ny), lax.rem(y + ny - 1, ny), lax.rem(y + 2, ny)
    right, left, sibling = y_right * 2 + core, y_left * 2 + core, y * 2 + 1 - core
    blocks, block = q_v.shape[0], q_v.shape[1]
    chunk = spread_v.shape[1]
    width = sib_v.shape[2]
    half = width // 2
    heads = q_v.shape[2] // HEAD_DIM
    tiles = score_v.shape[0] - 1
    per_tile = n // tiles

    def load(j, what, src, dst):
        return pltpu.make_async_copy(src, dst, in_sem.at[j, what])

    def own_loads(j):
        rows = pl.ds(j * block, block)
        return [
            load(j, 0, q_hbm.at[rows], q_v.at[j]),
            load(j, 1, do_hbm.at[rows], do_v.at[j]),
            load(j, 2, rk_hbm.at[rows], own_v.at[j, :, pl.ds(0, HEAD_DIM)]),
            load(j, 3, rv_hbm.at[rows], own_v.at[j, :, pl.ds(HEAD_DIM, HEAD_DIM)]),
        ]

    def w_load(dest):
        rows = pl.ds(pl.multiple_of(dest * width, width), width)
        return pltpu.make_async_copy(w_hbm.at[rows], w_v.at[rows], w_sem.at[dest])

    for j in range(blocks):
        for copy in own_loads(j):
            copy.start()

    barrier = pltpu.get_barrier_semaphore()

    def greet(o, carry):
        pl.semaphore_signal(
            barrier, inc=1, device_id={"dp": lax.rem(me + o, n)}, device_id_type=MESH
        )
        return carry

    lax.fori_loop(1, n, greet, 0)
    for other in (right, left, sibling):
        pl.semaphore_signal(barrier, inc=1, device_id={"mp": other}, device_id_type=MESH)
    for j in range(blocks):
        tile_v[j] = jnp.full((GROUP, HEAD_DIM), prompt_ref[j], jnp.int32).astype(F32).astype(BF16)
    pl.semaphore_wait(barrier, n - 1 + 3)

    def spread(o, carry):
        peer = lax.rem(me + o, n)
        rows = pl.ds(pl.multiple_of(peer * chunk, chunk), chunk)
        pltpu.make_async_remote_copy(
            src_ref=tile_v,
            dst_ref=table_v.at[me],
            send_sem=t_send,
            recv_sem=t_recv,
            device_id={"dp": peer},
            device_id_type=MESH,
        ).start()
        for what, src in ((0, pk_hbm), (1, pv_hbm)):
            pltpu.make_async_remote_copy(
                src_ref=src.at[rows],
                dst_ref=spread_v.at[me, :, pl.ds(what * HEAD_DIM, HEAD_DIM)],
                send_sem=s1_send,
                recv_sem=s1_recv,
                device_id={"dp": peer},
                device_id_type=MESH,
            ).start()
        return carry

    lax.fori_loop(1, n, spread, 0)
    mine = pl.ds(pl.multiple_of(me * chunk, chunk), chunk)
    pltpu.make_async_copy(tile_v, table_v.at[me], t_recv).start()
    for what, src in ((0, pk_hbm), (1, pv_hbm)):
        pltpu.make_async_copy(
            src.at[mine], spread_v.at[me, :, pl.ds(what * HEAD_DIM, HEAD_DIM)], s1_recv
        ).start()
    for dest in range(nmp):
        w_load(dest).start()

    pltpu.make_async_copy(table_v, table_v, t_recv).wait()
    side = n * GROUP
    row = lax.broadcasted_iota(jnp.int32, (side, side), 0)
    col = lax.broadcasted_iota(jnp.int32, (side, side), 1)
    same = lax.rem(row, GROUP) == lax.rem(col, GROUP)
    prompt_of_col = (col // GROUP).astype(F32)
    for j in range(blocks):
        wanted = table_v[:, j].reshape(side, HEAD_DIM).astype(F32)
        if side > HEAD_DIM:
            wanted = jnp.concatenate([wanted] * (side // HEAD_DIM), axis=1)
        else:
            wanted = wanted[:, :side]
        choose_v[j] = jnp.where(same & (wanted == prompt_of_col), 1.0, 0.0).astype(BF16)

    pltpu.make_async_copy(spread_v, spread_v, s1_recv).wait()
    for j in range(blocks):
        for g in range(chunk // GROUP):
            rows = pl.ds(g * GROUP, GROUP)
            picked = dot(choose_v[j], spread_v[:, rows, :].reshape(side, 2 * HEAD_DIM))
            send_v[j, :, rows, :] = picked.astype(BF16).reshape(n, GROUP, 2 * HEAD_DIM)

        def deliver(o, carry):
            peer = lax.rem(me + o, n)
            pltpu.make_async_remote_copy(
                src_ref=send_v.at[j, peer],
                dst_ref=pre_v.at[j, me],
                send_sem=s2_send.at[j],
                recv_sem=s2_recv.at[j],
                device_id={"dp": peer},
                device_id_type=MESH,
            ).start()
            return carry

        lax.fori_loop(1, n, deliver, 0)
        pltpu.make_async_copy(send_v.at[j, me], pre_v.at[j, me], s2_recv.at[j]).start()

    key_cols, value_cols = pl.ds(0, HEAD_DIM), pl.ds(HEAD_DIM, HEAD_DIM)

    def part_of(j, t, cols):
        if t == tiles:
            return own_v[j, :, cols]
        got = pre_v[j, t * per_tile : (t + 1) * per_tile, :, cols]
        return got.reshape(block, HEAD_DIM)

    def visible(j):
        place = lax.broadcasted_iota(jnp.int32, (block, block), 1)
        key = lax.broadcasted_iota(jnp.int32, (block, block), 0)
        end = lengths_ref[j, 0]
        first = jnp.where(place >= end, end, 0)
        for s in range(1, lengths_ref.shape[1] - 1):
            end = end + lengths_ref[j, s]
            first = jnp.where(place >= end, end, first)
        return (key >= first) & (key <= place)

    def prepare(j):
        for copy in own_loads(j):
            copy.wait()
        pltpu.make_async_copy(pre_v.at[j], pre_v.at[j], s2_recv.at[j]).wait()
        for t in range(tiles + 1):
            keys_t[:, t * block : (t + 1) * block] = part_of(j, t, key_cols).T
        grad_v[...] = jnp.zeros_like(grad_v)

    def attend(j, lower, upper):
        def head(h, carry):
            cols = pl.ds(pl.multiple_of(h * HEAD_DIM, HEAD_DIM), HEAD_DIM)
            qh, doh = q_v[j, :, cols], do_v[j, :, cols]
            top = None
            for t in range(tiles + 1):
                s = dot_nt(part_of(j, t, key_cols), qh)
                if t == tiles:
                    s = jnp.where(visible(j), s, -1e30)
                score_v[t] = s
                got = fold(s, jnp.max)
                top = got if top is None else jnp.maximum(top, got)
            top = jnp.max(top, axis=0, keepdims=True)
            total = jnp.zeros((8, block), F32)
            mixed = jnp.zeros((8, block), F32)
            for t in range(tiles + 1):
                dp = dot_nt(part_of(j, t, value_cols), doh)
                dprob_v[t] = dp
                e = jnp.exp2((score_v[t] - top) * (SCALE * LOG2E))
                score_v[t] = e
                total += fold(e, jnp.sum)
                mixed += fold(e * dp, jnp.sum)
            inverse = 1.0 / jnp.sum(total, axis=0, keepdims=True)
            delta = jnp.sum(mixed, axis=0, keepdims=True) * inverse
            dq = jnp.zeros((HEAD_DIM, block), F32)
            for t in range(tiles + 1):
                prob = score_v[t] * inverse
                ds = (prob * (dprob_v[t] - delta)).astype(BF16)
                grad_v[t, :, key_cols] += dot(ds, qh)
                grad_v[t, :, value_cols] += dot(prob.astype(BF16), doh)
                dq += dot(keys_t[:, t * block : (t + 1) * block], ds)
            qg_v[j, cols, :] = (dq * SCALE).astype(BF16)
            return carry

        lax.fori_loop(lower, upper, head, 0)

    def rounded(t):
        return jnp.concatenate(
            [grad_v[t, :, key_cols] * SCALE, grad_v[t, :, value_cols]], axis=1
        ).astype(BF16)

    def give_back(j):
        for t in range(tiles):
            back_v[j, t * per_tile : (t + 1) * per_tile] = rounded(t).reshape(
                per_tile, chunk, 2 * HEAD_DIM
            )
        ownout_v[j] = rounded(tiles)
        pltpu.make_async_copy(
            ownout_v.at[j], own_hbm.at[pl.ds(j * block, block)], out_sem.at[j, 0]
        ).start()

        def deliver(o, carry):
            peer = lax.rem(me + o, n)
            pltpu.make_async_remote_copy(
                src_ref=back_v.at[j, peer],
                dst_ref=gather_v.at[j, me],
                send_sem=b_send.at[j],
                recv_sem=b_recv.at[j],
                device_id={"dp": peer},
                device_id_type=MESH,
            ).start()
            return carry

        lax.fori_loop(1, n, deliver, 0)
        pltpu.make_async_copy(back_v.at[j, me], gather_v.at[j, me], b_recv.at[j]).start()

    def bring_home():
        for j in range(blocks):
            pltpu.make_async_copy(gather_v.at[j], gather_v.at[j], b_recv.at[j]).wait()
        pick = [choose_v[j].astype(F32).T.astype(BF16) for j in range(blocks)]
        for g in range(chunk // GROUP):
            rows = pl.ds(g * GROUP, GROUP)
            added = jnp.zeros((side, 2 * HEAD_DIM), F32)
            for j in range(blocks):
                added += dot(pick[j], gather_v[j, :, rows, :].reshape(side, 2 * HEAD_DIM))
            home_v[:, rows, :] = added.astype(BF16).reshape(n, GROUP, 2 * HEAD_DIM)

        def deliver(o, carry):
            peer = lax.rem(me + o, n)
            pltpu.make_async_remote_copy(
                src_ref=home_v.at[peer],
                dst_ref=pre_hbm.at[me],
                send_sem=h_send,
                recv_sem=h_recv,
                device_id={"dp": peer},
                device_id_type=MESH,
            ).start()
            return carry

        lax.fori_loop(1, n, deliver, 0)
        pltpu.make_async_copy(home_v.at[me], pre_hbm.at[me], h_recv).start()

    def project(j, dest):
        if j == 0:
            w_load(dest).wait()
        step = min(512, width)

        def tile(i, carry):
            rows = pl.ds(pl.multiple_of(i * step, step), step)
            from_w = pl.ds(pl.multiple_of(dest * width + i * step, step), step)
            part_v[j, dest, rows, :] = dot(w_v[from_w, :], qg_v[j]).astype(BF16)
            return carry

        lax.fori_loop(0, width // step, tile, 0)

    def to_sibling(j, y_dest, slot):
        return pltpu.make_async_remote_copy(
            src_ref=part_v.at[j, y_dest * 2 + 1 - core],
            dst_ref=sib_v.at[j, slot],
            send_sem=sib_send.at[j, slot],
            recv_sem=sib_recv.at[j, slot],
            device_id={"mp": sibling},
            device_id_type=MESH,
        )

    def remote(src, dst, send, recv, dest):
        return pltpu.make_async_remote_copy(
            src_ref=src,
            dst_ref=dst,
            send_sem=send,
            recv_sem=recv,
            device_id={"mp": dest},
            device_id_type=MESH,
        )

    halves, ways = (pl.ds(0, half), pl.ds(half, half)), (right, left)

    def opposite(j, way):
        src = opp_v.at[j, halves[way]]
        return remote(src, hop_v.at[j, way], opp_send.at[j, way], opp_recv.at[j, way], ways[way])

    def raw(j, way):
        rows = halves[1 - way]
        src, dst = near_v.at[j, way, rows], side_v.at[j, way, rows]
        return remote(src, dst, raw_send.at[j, way], raw_recv.at[j, way], ways[way])

    def mixed(j, way):
        rows = halves[way]
        src, dst = near_v.at[j, way, rows], side_v.at[j, way, rows]
        return remote(src, dst, mix_send.at[j, way], mix_recv.at[j, way], ways[way])

    def chip_sum(j, y_dest, slot, rows):
        mine = part_v[j, y_dest * 2 + core, rows, :].astype(F32)
        return mine + sib_v[j, slot, rows, :].astype(F32)

    def send_partials(j):
        project(j, y_opp * 2 + 1 - core)
        to_sibling(j, y_opp, 0).start()
        project(j, y_opp * 2 + core)
        project(j, y_right * 2 + 1 - core)
        to_sibling(j, y_right, 1).start()
        to_sibling(j, y_opp, 0).wait_recv()
        opp_v[j] = chip_sum(j, y_opp, 0, slice(None)).astype(BF16)
        for way in range(2):
            opposite(j, way).start()
        project(j, y_left * 2 + 1 - core)
        to_sibling(j, y_left, 2).start()
        project(j, y_right * 2 + core)
        to_sibling(j, y_right, 1).wait_recv()
        near_v[j, 0] = chip_sum(j, y_right, 1, slice(None)).astype(BF16)
        raw(j, 0).start()
        project(j, y_left * 2 + core)
        to_sibling(j, y_left, 2).wait_recv()
        near_v[j, 1] = chip_sum(j, y_left, 2, slice(None)).astype(BF16)
        raw(j, 1).start()
        project(j, y * 2 + 1 - core)
        to_sibling(j, y, 3).start()
        project(j, y * 2 + core)

    def pass_on(j):
        for way, rows in enumerate(halves):
            opposite(j, way).wait_recv()
            near_v[j, way, rows, :] = (
                near_v[j, way, rows, :].astype(F32) + hop_v[j, way].astype(F32)
            ).astype(BF16)
            mixed(j, way).start()

    def finish(j):
        to_sibling(j, y, 3).wait_recv()
        for way in range(2):
            raw(j, way).wait_recv()
            mixed(j, way).wait_recv()
        added = chip_sum(j, y, 3, slice(None))
        added += side_v[j, 0].astype(F32) + side_v[j, 1].astype(F32)
        sum_v[j] = added.astype(BF16)
        pltpu.make_async_copy(
            sum_v.at[j], out_hbm.at[:, pl.ds(j * block, block)], out_sem.at[j, 1]
        ).start()

    prepare(0)
    attend(0, 0, heads)
    give_back(0)
    send_partials(0)
    prepare(1)
    attend(1, 0, heads // 2)
    pass_on(0)
    attend(1, heads // 2, heads)
    give_back(1)
    send_partials(1)
    bring_home()
    pass_on(1)
    finish(0)
    finish(1)

    def all_but_one(ref, sem):
        part = ref.at[pl.ds(0, n - 1)]
        pltpu.make_async_copy(part, part, sem).wait()

    all_but_one(table_v, t_send)
    all_but_one(spread_v, s1_send)
    all_but_one(home_v, h_send)
    for j in range(blocks):
        all_but_one(send_v.at[j], s2_send.at[j])
        all_but_one(back_v.at[j], b_send.at[j])
        for slot, y_dest in enumerate((y_opp, y_right, y_left, y)):
            to_sibling(j, y_dest, slot).wait_send()
        for way in range(2):
            opposite(j, way).wait_send()
            raw(j, way).wait_send()
            mixed(j, way).wait_send()
        pltpu.make_async_copy(
            ownout_v.at[j], own_hbm.at[pl.ds(j * block, block)], out_sem.at[j, 0]
        ).wait()
        pltpu.make_async_copy(
            sum_v.at[j], out_hbm.at[:, pl.ds(j * block, block)], out_sem.at[j, 1]
        ).wait()
    pltpu.make_async_copy(pre_hbm, pre_hbm, h_recv).wait()


def shards(
    queries,
    out_grad,
    response_keys,
    response_values,
    prefix_keys,
    prefix_values,
    q_weight,
    block_prompt,
    response_lengths,
):
    n, nmp = lax.axis_size("dp"), lax.axis_size("mp")
    blocks = block_prompt.shape[0]
    rows, cols = queries.shape
    block = rows // blocks
    prefix = prefix_keys.shape[0]
    chunk = prefix // n
    tiles = prefix // block
    width = q_weight.shape[0] // nmp
    two = 2 * HEAD_DIM
    dma = pltpu.SemaphoreType.DMA
    any_space = pl.BlockSpec(memory_space=pl.ANY)
    smem = pl.BlockSpec(memory_space=pltpu.SMEM)
    flops = 2 * rows * cols * (5 * (prefix + block) + q_weight.shape[0])
    out, own, pre = pl.pallas_call(
        functools.partial(kernel, n, nmp),
        out_shape=(
            jax.ShapeDtypeStruct((width, rows), BF16),
            jax.ShapeDtypeStruct((rows, two), BF16),
            jax.ShapeDtypeStruct((n, chunk, two), BF16),
        ),
        in_specs=[smem, smem] + [any_space] * 7,
        out_specs=(any_space,) * 3,
        scratch_shapes=[
            pltpu.VMEM((blocks, block, cols), BF16),
            pltpu.VMEM((blocks, block, cols), BF16),
            pltpu.VMEM((blocks, block, two), BF16),
            pltpu.VMEM(q_weight.shape, BF16),
            pltpu.VMEM((blocks, GROUP, HEAD_DIM), BF16),
            pltpu.VMEM((n, blocks, GROUP, HEAD_DIM), BF16),
            pltpu.VMEM((n, chunk, two), BF16),
            pltpu.VMEM((blocks, n * GROUP, n * GROUP), BF16),
            pltpu.VMEM((blocks, n, chunk, two), BF16),
            pltpu.VMEM((blocks, n, chunk, two), BF16),
            pltpu.VMEM((HEAD_DIM, prefix + block), BF16),
            pltpu.VMEM((tiles + 1, block, block), F32),
            pltpu.VMEM((tiles + 1, block, block), F32),
            pltpu.VMEM((tiles + 1, block, two), F32),
            pltpu.VMEM((blocks, cols, block), BF16),
            pltpu.VMEM((blocks, block, two), BF16),
            pltpu.VMEM((blocks, n, chunk, two), BF16),
            pltpu.VMEM((blocks, n, chunk, two), BF16),
            pltpu.VMEM((n, chunk, two), BF16),
            pltpu.VMEM((blocks, nmp, width, block), BF16),
            pltpu.VMEM((blocks, nmp // 2, width, block), BF16),
            pltpu.VMEM((blocks, width, block), BF16),
            pltpu.VMEM((blocks, 2, width // 2, block), BF16),
            pltpu.VMEM((blocks, 2, width, block), BF16),
            pltpu.VMEM((blocks, 2, width, block), BF16),
            pltpu.VMEM((blocks, width, block), BF16),
            dma((blocks, 4)),
            dma((nmp,)),
            dma,
            dma,
            dma,
            dma,
            dma((blocks,)),
            dma((blocks,)),
            dma((blocks,)),
            dma((blocks,)),
            dma,
            dma,
            dma((blocks, 4)),
            dma((blocks, 4)),
            dma((blocks, 2)),
            dma((blocks, 2)),
            dma((blocks, 2)),
            dma((blocks, 2)),
            dma((blocks, 2)),
            dma((blocks, 2)),
            dma((blocks, 2)),
        ],
        compiler_params=pltpu.CompilerParams(
            collective_id=0, has_side_effects=True, vmem_limit_bytes=60 * 2**20
        ),
        cost_estimate=pl.CostEstimate(
            flops=flops, bytes_accessed=2 * q_weight.size, transcendentals=0
        ),
        name="attention_backward",
    )(
        block_prompt,
        response_lengths,
        queries,
        out_grad,
        response_keys,
        response_values,
        prefix_keys,
        prefix_values,
        q_weight,
    )
    pre = pre.reshape(prefix, two)
    return (
        out.T,
        own[:, :HEAD_DIM],
        own[:, HEAD_DIM:],
        pre[:, :HEAD_DIM],
        pre[:, HEAD_DIM:],
    )


def solution(mesh):
    return jax.shard_map(
        shards,
        mesh=mesh,
        in_specs=(
            P("dp", "mp"),
            P("dp", "mp"),
            P("dp", "mp"),
            P("dp", "mp"),
            P("dp", "mp"),
            P("dp", "mp"),
            P(None, "mp"),
            P("dp"),
            P("dp", None),
        ),
        out_specs=(P("dp", "mp"), P("dp", "mp"), P("dp", "mp"), P("dp", "mp"), P("dp", "mp")),
        check_vma=False,
    )
```

time: 342 us -> 93 us (0.27)
  waiting for transfers between devices: 227 us -> 0 us
  Pallas kernels: 0 us -> 86.4 us
  matrix products: 72.1 us -> 0 us
  between operations: 15.7 us -> 0.64 us
  other arithmetic: 11 us -> 0 us
  local copies, waits for them, and re-layouts: 15.1 us -> 5.8 us
    reduce_scatter x3 -> x0, waiting for transfers between devices: 145 us -> none  [the longest x1 81.2 us: shards(): lax.psum_scatter(table_k.astype(jnp.bfloat16), 'dp', scatter_dimension=0,...]
    pallas_call x0 -> x1, Pallas kernels: none -> 86.4 us  [shards(): pl.pallas_call(functools.partial(kernel, n, nmp), out_shape=(jax.ShapeDty...]
    all_gather x2 -> x0, waiting for transfers between devices: 80.8 us -> none  [the longest x1 47.6 us: shards(): lax.all_gather(prefix_keys, 'dp', axis=0, tiled=True)]
    dot_general x13 -> x0, matrix products: 72.1 us -> none  [the longest x1 30.6 us: shards(): lax.dot_general(q_weight, flat_grad, (((1,), (1,)), ((), ())), preferred_...]
    reduce_sum x4 -> x0, other arithmetic: 4.48 us -> none  [the longest x2 4.31 us: block_grads(): prob = expo / jnp.sum(expo, axis=-1, keepdims=True)]
    convert_element_type x2 -> x0, other arithmetic: 4.47 us -> none  [the longest x1 2.26 us: shards(): table_v.astype(jnp.bfloat16)]
  transfers between devices with their start and end apart: 5 -> 0, of which waited for: 5 -> 0; matrix products, arithmetic and copies ran while one was open for 28% -> 0% of each run, Pallas kernels for 0% -> 0%
where the time goes in v1:
time: 93 us; the launch traced here: 92.8 us
  Pallas kernels  86.4 us (93%)
  local copies, waits for them, and re-layouts  5.8 us (6%)
    pallas_call x1, Pallas kernels, shards(): pl.pallas_call(functools.partial(kernel, n, nmp), out_shape=(jax.ShapeDty...  86.4 us
    unnamed x1, local copies, waits for them, and re-layouts  2.27 us

profile of v1, /device:TPU:1, one launch (start us, length us, event | category | flops | bytes accessed | tf_op | source)
XLA Modules:
  0.0 92.8 jit_solution(13399984088523097190)
XLA Ops:
  0.6 86.4 %attention_backward.1 = (bf16[1024,512]{1,0:T(8,128)(2,1)}, bf16[512,256]{1,0:T(8,128)(2,1)}, bf16[16,64,256]{2,1,0:T(8,128)(2,1)}) custom-call(s32[2]{0:T(128)} %prompt_ref.1, s32[2,4]{1,0:T(2,128)} %lengths_ref.1, bf16[512,1024]{1,0:T(8,128)(2,1)} %q_hbm.1, bf16[512,1024]{1,0:T(8,128)(2,1)} %do_hbm.1, bf16[512,128]{1,0:T(8,128)(2,1)} %rk_hbm.1, ...), custom_call_target="tpu_custom_call" | custom-call | flops 15300820992 | bytes 16777216 | tf_op jit(solution)/shard_map/attention_backward/pallas_call | solution.py:491
  87.0 2.3 %copy.14 = bf16[512,1024]{1,0:T(8,128)(2,1)} copy(bf16[512,1024]{0,1:T(8,128)(2,1)} %bitcast.2) | data formatting | bytes 2097152
  89.3 1.7 %fusion.1 = (bf16[512,128]{1,0:T(8,128)(2,1)}, bf16[512,128]{1,0:T(8,128)(2,1)}) fusion(bf16[512,256]{1,0:T(8,128)(2,1)} %get-tuple-element.9), kind=kLoop, calls=%fused_computation.1 | loop fusion | bytes 524288 | tf_op jit(solution)/shard_map/slice | solution.py:571
  91.0 1.9 %fusion = (bf16[1024,128]{1,0:T(8,128)(2,1)}, bf16[1024,128]{1,0:T(8,128)(2,1)}) fusion(bf16[1024,256]{1,0:T(8,128)(2,1)} %bitcast.3), kind=kLoop, calls=%fused_computation | loop fusion | bytes 1048576 | tf_op jit(solution)/shard_map/slice | solution.py:573

commit v2 on v1

v2 whole, which is shorter than its diff:
```python
import functools

import jax
import jax.numpy as jnp
from jax import lax
from jax.experimental import pallas as pl
from jax.experimental.pallas import tpu as pltpu
from jax.sharding import PartitionSpec as P

HEAD_DIM = 128
GROUP = 16
SCALE = HEAD_DIM ** (-0.5)
LOG2E = 1.4426950408889634
MESH = pl.DeviceIdType.MESH
F32 = jnp.float32
BF16 = jnp.bfloat16


def dot(a, b):
    return jnp.dot(a, b, preferred_element_type=F32)


def dot_nt(a, b):
    return lax.dot_general(a, b, (((1,), (1,)), ((), ())), preferred_element_type=F32)


def fold(x, op):
    rows, cols = x.shape
    return op(x.reshape(rows // 8, 8, cols), axis=0)


def kernel(
    n,
    nmp,
    prompt_ref,
    lengths_ref,
    q_hbm,
    do_hbm,
    rk_hbm,
    rv_hbm,
    pk_hbm,
    pv_hbm,
    w_hbm,
    out_hbm,
    own_hbm,
    pre_hbm,
    q_v,
    do_v,
    own_v,
    w_v,
    table_v,
    stage_v,
    spread_v,
    choose_v,
    send_v,
    pre_v,
    keys_t,
    score_v,
    dprob_v,
    mask_v,
    grad_v,
    qg_v,
    ownout_v,
    back_v,
    gather_v,
    home_v,
    part_v,
    sib_v,
    hop_v,
    side_v,
    sum_v,
    in_sem,
    w_sem,
    t_send,
    t_recv,
    s1_sem,
    s1_send,
    s1_recv,
    s2_send,
    s2_recv,
    b_send,
    b_recv,
    h_send,
    h_recv,
    sib_send,
    sib_recv,
    opp_send,
    opp_recv,
    raw_send,
    raw_recv,
    mix_send,
    mix_recv,
    out_sem,
):
    me = lax.axis_index("dp")
    mp = lax.axis_index("mp")
    ny = nmp // 2
    y, core = mp // 2, lax.rem(mp, 2)
    y_right, y_left, y_opp = lax.rem(y + 1, ny), lax.rem(y + ny - 1, ny), lax.rem(y + 2, ny)
    right, left, sibling = y_right * 2 + core, y_left * 2 + core, y * 2 + 1 - core
    blocks, block = q_v.shape[0], q_v.shape[1]
    chunk = send_v.shape[2]
    width = sib_v.shape[2]
    half = width // 2
    heads = q_v.shape[2] // HEAD_DIM
    tiles = score_v.shape[1] - 1
    per_tile = n // tiles

    def load(j, what, src, dst):
        return pltpu.make_async_copy(src, dst, in_sem.at[j, what])

    def own_loads(j):
        rows = pl.ds(j * block, block)
        return [
            load(j, 0, q_hbm.at[rows], q_v.at[j]),
            load(j, 1, do_hbm.at[rows], do_v.at[j]),
            load(j, 2, rk_hbm.at[rows], own_v.at[j, :, pl.ds(0, HEAD_DIM)]),
            load(j, 3, rv_hbm.at[rows], own_v.at[j, :, pl.ds(HEAD_DIM, HEAD_DIM)]),
        ]

    def w_load(dest):
        rows = pl.ds(pl.multiple_of(dest * width, width), width)
        return pltpu.make_async_copy(w_hbm.at[rows], w_v.at[rows], w_sem.at[dest])

    key_cols, value_cols = pl.ds(0, HEAD_DIM), pl.ds(HEAD_DIM, HEAD_DIM)
    side = n * GROUP

    def prompt_loads():
        return [
            pltpu.make_async_copy(src, stage_v.at[:, :, cols], s1_sem.at[what])
            for what, src, cols in ((0, pk_hbm, key_cols), (1, pv_hbm, value_cols))
        ]

    for copy in prompt_loads():
        copy.start()
    for j in range(blocks):
        for copy in own_loads(j):
            copy.start()

    side_x = 4 if n == 16 else n
    if n == 16:
        ones = [(0, 1), (0, 3), (1, 0), (3, 0), (1, 1), (3, 3), (1, 3), (3, 1)]
        offsets = ones + [(0, 2), (2, 0), (1, 2), (3, 2), (2, 1), (2, 3), (2, 2)]
    else:
        offsets = [(0, o) for o in range(1, n)]
    side_z = n // side_x
    my_z, my_x = me // side_x, lax.rem(me, side_x)
    peers = [
        lax.rem(my_z + dz, side_z) * side_x + lax.rem(my_x + dx, side_x) for dz, dx in offsets
    ]

    barrier = pltpu.get_barrier_semaphore()
    for peer in peers:
        pl.semaphore_signal(barrier, inc=1, device_id={"dp": peer}, device_id_type=MESH)
    for other in (right, left, sibling):
        pl.semaphore_signal(barrier, inc=1, device_id={"mp": other}, device_id_type=MESH)
    for j in range(blocks):
        table_v[me, j, :] = jnp.full((HEAD_DIM,), prompt_ref[j], jnp.int32)
    for copy in prompt_loads():
        copy.wait()
    pl.semaphore_wait(barrier, n - 1 + 3)

    def to_all(src, dst, send, recv):
        for peer in peers:
            pltpu.make_async_remote_copy(
                src_ref=src.at[peer],
                dst_ref=dst.at[me],
                send_sem=send,
                recv_sem=recv,
                device_id={"dp": peer},
                device_id_type=MESH,
            ).start()
        pltpu.make_async_copy(src.at[me], dst.at[me], recv).start()

    def load_weights():
        for dest in range(nmp):
            w_load(dest).start()

    def pick(j):
        for g in range(chunk // GROUP):
            rows = pl.ds(g * GROUP, GROUP)
            picked = dot(choose_v[j], spread_v[:, rows, :].reshape(side, 2 * HEAD_DIM))
            send_v[j, :, rows, :] = picked.astype(BF16).reshape(n, GROUP, 2 * HEAD_DIM)

    def fetch():
        for peer in peers:
            pltpu.make_async_remote_copy(
                src_ref=table_v.at[me],
                dst_ref=table_v.at[me],
                send_sem=t_send,
                recv_sem=t_recv,
                device_id={"dp": peer},
                device_id_type=MESH,
            ).start()
        to_all(stage_v, spread_v, s1_send, s1_recv)
        load_weights()
        row = lax.broadcasted_iota(jnp.int32, (side, side), 0)
        col = lax.broadcasted_iota(jnp.int32, (side, side), 1)
        same = lax.rem(row, GROUP) == lax.rem(col, GROUP)
        prompt_of_col = jnp.where(same, col // GROUP, -1)
        others = table_v.at[pl.ds(0, n - 1)]
        pltpu.make_async_copy(others, others, t_recv).wait()

        for j in range(blocks):
            wanted = jnp.broadcast_to(table_v[:, j : j + 1, :], (n, GROUP, HEAD_DIM))
            wanted = wanted.reshape(side, HEAD_DIM)
            if side > HEAD_DIM:
                wanted = jnp.concatenate([wanted] * (side // HEAD_DIM), axis=1)
            else:
                wanted = wanted[:, :side]
            choose_v[j] = jnp.where(wanted == prompt_of_col, 1.0, 0.0).astype(BF16)

        pltpu.make_async_copy(spread_v, spread_v, s1_recv).wait()
        for j in range(blocks):
            pick(j)
            if j == 0:
                to_all(send_v.at[j], pre_v.at[j], s2_send.at[j], s2_recv.at[j])

    def part_of(j, t, cols):
        if t == tiles:
            return own_v[j, :, cols]
        got = pre_v[j, t * per_tile : (t + 1) * per_tile, :, cols]
        return got.reshape(block, HEAD_DIM)

    def visible(j):
        place = lax.broadcasted_iota(jnp.int32, (block, block), 1)
        key = lax.broadcasted_iota(jnp.int32, (block, block), 0)
        end = lengths_ref[j, 0]
        first = jnp.where(place >= end, end, 0)
        for s in range(1, lengths_ref.shape[1] - 1):
            end = end + lengths_ref[j, s]
            first = jnp.where(place >= end, end, first)
        return (key >= first) & (key <= place)

    def prepare(j):
        for copy in own_loads(j):
            copy.wait()
        pltpu.make_async_copy(pre_v.at[j], pre_v.at[j], s2_recv.at[j]).wait()
        if j + 1 < blocks:
            to_all(send_v.at[j + 1], pre_v.at[j + 1], s2_send.at[j + 1], s2_recv.at[j + 1])
        for t in range(tiles + 1):
            keys_t[:, t * block : (t + 1) * block] = part_of(j, t, key_cols).T
        grad_v[...] = jnp.zeros_like(grad_v)
        mask_v[...] = jnp.where(visible(j), 0.0, -1e30)

    def attend(j, lower, upper):
        per = 4

        def scores(h, slot):
            cols = pl.ds(pl.multiple_of(h * HEAD_DIM, HEAD_DIM), HEAD_DIM)
            qh = q_v[j, :, cols]
            top = None
            for t in range(tiles + 1):
                s = dot_nt(part_of(j, t, key_cols), qh)
                if t == tiles:
                    s = s + mask_v[...]
                score_v[slot, t] = s
                got = fold(s, jnp.max)
                top = got if top is None else jnp.maximum(top, got)
            return jnp.max(top, axis=0, keepdims=True)

        def middle(h, slot, top):
            cols = pl.ds(pl.multiple_of(h * HEAD_DIM, HEAD_DIM), HEAD_DIM)
            doh = do_v[j, :, cols]
            total = jnp.zeros((8, block), F32)
            mixed = jnp.zeros((8, block), F32)
            for t in range(tiles + 1):
                dp = dot_nt(part_of(j, t, value_cols), doh)
                dprob_v[slot, t] = dp
                e = jnp.exp2((score_v[slot, t] - top) * (SCALE * LOG2E))
                score_v[slot, t] = e
                total += fold(e, jnp.sum)
                mixed += fold(e * dp, jnp.sum)
            inverse = 1.0 / jnp.sum(total, axis=0, keepdims=True)
            delta = jnp.sum(mixed, axis=0, keepdims=True) * inverse
            return inverse, delta

        def grads(hs, stats):
            colss = [pl.ds(pl.multiple_of(h * HEAD_DIM, HEAD_DIM), HEAD_DIM) for h in hs]
            qs = jnp.concatenate([q_v[j, :, c] for c in colss], axis=0)
            dos = jnp.concatenate([do_v[j, :, c] for c in colss], axis=0)
            dqs = [jnp.zeros((HEAD_DIM, block), F32) for _ in hs]
            for t in range(tiles + 1):
                dss, ps = [], []
                for slot, (inverse, delta) in enumerate(stats):
                    prob = score_v[slot, t] * inverse
                    ds = (prob * (dprob_v[slot, t] - delta)).astype(BF16)
                    dss.append(ds)
                    ps.append(prob.astype(BF16))
                    dqs[slot] += dot(keys_t[:, t * block : (t + 1) * block], ds)
                grad_v[t, :, key_cols] += dot(jnp.concatenate(dss, axis=1), qs)
                grad_v[t, :, value_cols] += dot(jnp.concatenate(ps, axis=1), dos)
            for c, dq in zip(colss, dqs):
                qg_v[j, c, :] = (dq * SCALE).astype(BF16)

        def step(i, carry):
            hs = [i * per + s for s in range(per)]
            tops = [scores(h, s) for s, h in enumerate(hs)]
            stats = [middle(h, s, top) for s, (h, top) in enumerate(zip(hs, tops))]
            grads(hs, stats)
            return carry

        lax.fori_loop(lower // per, upper // per, step, 0)

    def rounded(t):
        return jnp.concatenate(
            [grad_v[t, :, key_cols] * SCALE, grad_v[t, :, value_cols]], axis=1
        ).astype(BF16)

    def give_back(j):
        for t in range(tiles):
            back_v[j, t * per_tile : (t + 1) * per_tile] = rounded(t).reshape(
                per_tile, chunk, 2 * HEAD_DIM
            )
        ownout_v[j] = rounded(tiles)
        pltpu.make_async_copy(
            ownout_v.at[j], own_hbm.at[pl.ds(j * block, block)], out_sem.at[j, 0]
        ).start()

        to_all(back_v.at[j], gather_v.at[j], b_send.at[j], b_recv.at[j])

    def bring_home():
        for j in range(blocks):
            pltpu.make_async_copy(gather_v.at[j], gather_v.at[j], b_recv.at[j]).wait()
        chosen = [choose_v[j].astype(F32).T.astype(BF16) for j in range(blocks)]
        for g in range(chunk // GROUP):
            rows = pl.ds(g * GROUP, GROUP)
            added = jnp.zeros((side, 2 * HEAD_DIM), F32)
            for j in range(blocks):
                added += dot(chosen[j], gather_v[j, :, rows, :].reshape(side, 2 * HEAD_DIM))
            home_v[:, rows, :] = added.astype(BF16).reshape(n, GROUP, 2 * HEAD_DIM)

        to_all(home_v, pre_hbm, h_send, h_recv)

    def project(j, dest):
        if j == 0:
            w_load(dest).wait()
        step = min(512, width)

        def tile(i, carry):
            rows = pl.ds(pl.multiple_of(i * step, step), step)
            from_w = pl.ds(pl.multiple_of(dest * width + i * step, step), step)
            part_v[j, dest, rows, :] = dot(w_v[from_w, :], qg_v[j]).astype(BF16)
            return carry

        lax.fori_loop(0, width // step, tile, 0)

    def to_sibling(j, y_dest, slot):
        return pltpu.make_async_remote_copy(
            src_ref=part_v.at[j, y_dest * 2 + 1 - core],
            dst_ref=sib_v.at[j, slot],
            send_sem=sib_send.at[j, slot],
            recv_sem=sib_recv.at[j, slot],
            device_id={"mp": sibling},
            device_id_type=MESH,
        )

    def remote(src, dst, send, recv, dest):
        return pltpu.make_async_remote_copy(
            src_ref=src,
            dst_ref=dst,
            send_sem=send,
            recv_sem=recv,
            device_id={"mp": dest},
            device_id_type=MESH,
        )

    halves, ways = (pl.ds(0, half), pl.ds(half, half)), (right, left)
    pieces = 2
    piece = half // pieces

    def piece_rows(way, p):
        return pl.ds(way * half + p * piece, piece)

    def opposite(j, way, p):
        src = part_v.at[j, y_opp * 2 + core, piece_rows(way, p)]
        sems = opp_send.at[j, way, p], opp_recv.at[j, way, p]
        return remote(src, hop_v.at[j, way, pl.ds(p * piece, piece)], *sems, ways[way])

    def raw(j, way):
        rows = halves[1 - way]
        src, dst = part_v.at[j, ways[way], rows], side_v.at[j, way, rows]
        return remote(src, dst, raw_send.at[j, way], raw_recv.at[j, way], ways[way])

    def mixed(j, way, p):
        rows = piece_rows(way, p)
        src, dst = part_v.at[j, ways[way], rows], side_v.at[j, way, rows]
        return remote(src, dst, mix_send.at[j, way, p], mix_recv.at[j, way, p], ways[way])

    def add_sibling(j, y_dest, slot):
        mine = part_v[j, y_dest * 2 + core].astype(F32)
        part_v[j, y_dest * 2 + core] = (mine + sib_v[j, slot].astype(F32)).astype(BF16)

    def send_partials(j):
        project(j, y_opp * 2 + 1 - core)
        to_sibling(j, y_opp, 0).start()
        project(j, y_opp * 2 + core)
        project(j, y_right * 2 + 1 - core)
        to_sibling(j, y_right, 1).start()
        to_sibling(j, y_opp, 0).wait_recv()
        add_sibling(j, y_opp, 0)
        for p in range(pieces):
            for way in range(2):
                opposite(j, way, p).start()
        project(j, y_left * 2 + 1 - core)
        to_sibling(j, y_left, 2).start()
        project(j, y_right * 2 + core)
        project(j, y_left * 2 + core)
        to_sibling(j, y_right, 1).wait_recv()
        add_sibling(j, y_right, 1)
        raw(j, 0).start()
        project(j, y * 2 + 1 - core)
        to_sibling(j, y, 3).start()
        to_sibling(j, y_left, 2).wait_recv()
        add_sibling(j, y_left, 2)
        raw(j, 1).start()
        project(j, y * 2 + core)

    def pass_on(j, p):
        for way in range(2):
            opposite(j, way, p).wait_recv()
            rows = piece_rows(way, p)
            hop = hop_v[j, way, pl.ds(p * piece, piece), :].astype(F32)
            part_v[j, ways[way], rows, :] = (
                part_v[j, ways[way], rows, :].astype(F32) + hop
            ).astype(BF16)
            mixed(j, way, p).start()

    def out_copy(j, way, p):
        cols = piece_rows(way, p)
        rows = pl.ds(j * block, block)
        return pltpu.make_async_copy(
            sum_v.at[j, :, cols], out_hbm.at[rows, cols], out_sem.at[j, 1 + way * pieces + p]
        )

    def finish(j):
        to_sibling(j, y, 3).wait_recv()
        for way in range(2):
            raw(j, way).wait_recv()
        for p in range(pieces):
            for way in range(2):
                rows = piece_rows(way, p)
                added = part_v[j, y * 2 + core, rows, :].astype(F32)
                added += sib_v[j, 3, rows, :].astype(F32)
                added += side_v[j, 1 - way, rows, :].astype(F32)
                mixed(j, way, p).wait_recv()
                added += side_v[j, way, rows, :].astype(F32)
                sum_v[j, :, rows] = added.astype(BF16).T
                out_copy(j, way, p).start()

    def all_but_one(ref, sem):
        part = ref.at[pl.ds(0, n - 1)]
        pltpu.make_async_copy(part, part, sem).wait()

    def end_fetch():
        all_but_one(table_v, t_send)
        all_but_one(spread_v, s1_send)
        for j in range(blocks):
            all_but_one(send_v.at[j], s2_send.at[j])

    def end_back():
        all_but_one(home_v, h_send)
        for j in range(blocks):
            all_but_one(back_v.at[j], b_send.at[j])
            pltpu.make_async_copy(
                ownout_v.at[j], own_hbm.at[pl.ds(j * block, block)], out_sem.at[j, 0]
            ).wait()
        pltpu.make_async_copy(pre_hbm, pre_hbm, h_recv).wait()

    def end_sum(j):
        for slot, y_dest in enumerate((y_opp, y_right, y_left, y)):
            to_sibling(j, y_dest, slot).wait_send()
        for way in range(2):
            raw(j, way).wait_send()
            for p in range(pieces):
                opposite(j, way, p).wait_send()
                mixed(j, way, p).wait_send()
                out_copy(j, way, p).wait()

    fetch()
    prepare(0)
    attend(0, 0, heads)
    give_back(0)
    send_partials(0)
    prepare(1)
    attend(1, 0, heads // 2)
    pass_on(0, 0)
    pass_on(0, 1)
    attend(1, heads // 2, heads)
    give_back(1)
    send_partials(1)
    finish(0)
    bring_home()
    pass_on(1, 0)
    pass_on(1, 1)
    finish(1)
    end_fetch()
    end_back()
    for j in range(blocks):
        end_sum(j)


def results(out, own, pre, input_grad, key_grad, value_grad, pre_key_grad, pre_value_grad, *held):
    out_v, own_v, pre_v, load_sem, store_sem = held
    keys, values = pl.ds(0, HEAD_DIM), pl.ds(HEAD_DIM, HEAD_DIM)
    half = out.shape[0] // 2
    upper, lower = pl.ds(0, half), pl.ds(half, half)
    loads = [(out.at[r], out_v.at[r]) for r in (upper, lower)] + [(own, own_v), (pre, pre_v)]
    stores = [
        [(out_v.at[upper], input_grad.at[upper])],
        [(out_v.at[lower], input_grad.at[lower])],
        [(own_v.at[:, keys], key_grad), (own_v.at[:, values], value_grad)],
        [(pre_v.at[:, keys], pre_key_grad), (pre_v.at[:, values], pre_value_grad)],
    ]
    loads = [pltpu.make_async_copy(a, b, load_sem.at[i]) for i, (a, b) in enumerate(loads)]
    for copy in loads:
        copy.start()
    started = []
    for load, pairs in zip(loads, stores):
        load.wait()
        for a, b in pairs:
            copy = pltpu.make_async_copy(a, b, store_sem.at[len(started)])
            copy.start()
            started.append(copy)
    for copy in started:
        copy.wait()


def shards(
    queries,
    out_grad,
    response_keys,
    response_values,
    prefix_keys,
    prefix_values,
    q_weight,
    block_prompt,
    response_lengths,
):
    n, nmp = lax.axis_size("dp"), lax.axis_size("mp")
    blocks = block_prompt.shape[0]
    rows, cols = queries.shape
    block = rows // blocks
    prefix = prefix_keys.shape[0]
    chunk = prefix // n
    tiles = prefix // block
    width = q_weight.shape[0] // nmp
    two = 2 * HEAD_DIM
    dma = pltpu.SemaphoreType.DMA
    any_space = pl.BlockSpec(memory_space=pl.ANY)
    smem = pl.BlockSpec(memory_space=pltpu.SMEM)
    flops = 2 * rows * cols * (5 * (prefix + block) + q_weight.shape[0])
    out, own, pre = pl.pallas_call(
        functools.partial(kernel, n, nmp),
        out_shape=(
            jax.ShapeDtypeStruct((rows, width), BF16),
            jax.ShapeDtypeStruct((rows, two), BF16),
            jax.ShapeDtypeStruct((n, chunk, two), BF16),
        ),
        in_specs=[smem, smem] + [any_space] * 7,
        out_specs=(any_space,) * 3,
        scratch_shapes=[
            pltpu.VMEM((blocks, block, cols), BF16),
            pltpu.VMEM((blocks, block, cols), BF16),
            pltpu.VMEM((blocks, block, two), BF16),
            pltpu.VMEM(q_weight.shape, BF16),
            pltpu.VMEM((n, blocks, HEAD_DIM), jnp.int32),
            pltpu.VMEM((n, chunk, two), BF16),
            pltpu.VMEM((n, chunk, two), BF16),
            pltpu.VMEM((blocks, n * GROUP, n * GROUP), BF16),
            pltpu.VMEM((blocks, n, chunk, two), BF16),
            pltpu.VMEM((blocks, n, chunk, two), BF16),
            pltpu.VMEM((HEAD_DIM, prefix + block), BF16),
            pltpu.VMEM((4, tiles + 1, block, block), F32),
            pltpu.VMEM((4, tiles + 1, block, block), F32),
            pltpu.VMEM((block, block), F32),
            pltpu.VMEM((tiles + 1, block, two), F32),
            pltpu.VMEM((blocks, cols, block), BF16),
            pltpu.VMEM((blocks, block, two), BF16),
            pltpu.VMEM((blocks, n, chunk, two), BF16),
            pltpu.VMEM((blocks, n, chunk, two), BF16),
            pltpu.VMEM((n, chunk, two), BF16),
            pltpu.VMEM((blocks, nmp, width, block), BF16),
            pltpu.VMEM((blocks, nmp // 2, width, block), BF16),
            pltpu.VMEM((blocks, 2, width // 2, block), BF16),
            pltpu.VMEM((blocks, 2, width, block), BF16),
            pltpu.VMEM((blocks, block, width), BF16),
            dma((blocks, 4)),
            dma((nmp,)),
            dma,
            dma,
            dma((2,)),
            dma,
            dma,
            dma((blocks,)),
            dma((blocks,)),
            dma((blocks,)),
            dma((blocks,)),
            dma,
            dma,
            dma((blocks, 4)),
            dma((blocks, 4)),
            dma((blocks, 2, 2)),
            dma((blocks, 2, 2)),
            dma((blocks, 2)),
            dma((blocks, 2)),
            dma((blocks, 2, 2)),
            dma((blocks, 2, 2)),
            dma((blocks, 5)),
        ],
        compiler_params=pltpu.CompilerParams(
            collective_id=0, has_side_effects=True, vmem_limit_bytes=60 * 2**20
        ),
        cost_estimate=pl.CostEstimate(
            flops=flops, bytes_accessed=2 * q_weight.size, transcendentals=0
        ),
        name="attention_backward",
    )(
        block_prompt,
        response_lengths,
        queries,
        out_grad,
        response_keys,
        response_values,
        prefix_keys.reshape(n, chunk, HEAD_DIM),
        prefix_values.reshape(n, chunk, HEAD_DIM),
        q_weight,
    )
    return pl.pallas_call(
        results,
        out_shape=(
            jax.ShapeDtypeStruct((rows, width), BF16),
            jax.ShapeDtypeStruct((rows, HEAD_DIM), BF16),
            jax.ShapeDtypeStruct((rows, HEAD_DIM), BF16),
            jax.ShapeDtypeStruct((prefix, HEAD_DIM), BF16),
            jax.ShapeDtypeStruct((prefix, HEAD_DIM), BF16),
        ),
        in_specs=[any_space] * 3,
        out_specs=(any_space,) * 5,
        scratch_shapes=[
            pltpu.VMEM((rows, width), BF16),
            pltpu.VMEM((rows, two), BF16),
            pltpu.VMEM((prefix, two), BF16),
            dma((4,)),
            dma((6,)),
        ],
        compiler_params=pltpu.CompilerParams(vmem_limit_bytes=60 * 2**20),
        name="results",
    )(out, own, pre.reshape(prefix, two))


def solution(mesh):
    return jax.shard_map(
        shards,
        mesh=mesh,
        in_specs=(
            P("dp", "mp"),
            P("dp", "mp"),
            P("dp", "mp"),
            P("dp", "mp"),
            P("dp", "mp"),
            P("dp", "mp"),
            P(None, "mp"),
            P("dp"),
            P("dp", None),
        ),
        out_specs=(P("dp", "mp"), P("dp", "mp"), P("dp", "mp"), P("dp", "mp"), P("dp", "mp")),
        check_vma=False,
    )
```

time: 93 us -> 81.1 us (0.87)
  Pallas kernels: 86.4 us -> 80.1 us
  local copies, waits for them, and re-layouts: 5.8 us -> 0 us
    pallas_call x1, Pallas kernels: 86.4 us -> 77.8 us  [shards(): pl.pallas_call(functools.partial(kernel, n, nmp), out_shape=(jax.ShapeDty...]
    slice x2 -> x0, local copies, waits for them, and re-layouts: 3.53 us -> none  [the longest x1 1.85 us: shards(): pre[:, HEAD_DIM:]]
    pallas_call x0 -> x1, Pallas kernels: none -> 2.35 us  [shards(): pl.pallas_call(results, out_shape=(jax.ShapeDtypeStruct((rows, width), BF...]
    unnamed x1 -> x0, local copies, waits for them, and re-layouts: 2.27 us -> none
where the time goes in v2:
time: 81.1 us; the launch traced here: 80.9 us
  Pallas kernels  80.1 us (99%)
    pallas_call x1, Pallas kernels, shards(): pl.pallas_call(functools.partial(kernel, n, nmp), out_shape=(jax.ShapeDty...  77.8 us
    pallas_call x1, Pallas kernels, shards(): pl.pallas_call(results, out_shape=(jax.ShapeDtypeStruct((rows, width), BF...  2.35 us

profile of v2, /device:TPU:1, one launch (start us, length us, event | category | flops | bytes accessed | tf_op | source)
XLA Modules:
  0.0 80.9 jit_solution(4411799352905214931)
XLA Ops:
  0.6 77.8 %attention_backward.1 = (bf16[512,1024]{1,0:T(8,128)(2,1)}, bf16[512,256]{1,0:T(8,128)(2,1)}, bf16[16,64,256]{2,1,0:T(8,128)(2,1)}) custom-call(s32[2]{0:T(128)} %prompt_ref.1, s32[2,4]{1,0:T(2,128)} %lengths_ref.1, bf16[512,1024]{1,0:T(8,128)(2,1)} %q_hbm.1, bf16[512,1024]{1,0:T(8,128)(2,1)} %do_hbm.1, bf16[512,128]{1,0:T(8,128)(2,1)} %rk_hbm.1, ...), custom_call_target="tpu_custom_call" | custom-call | flops 15300820992 | bytes 16777216 | tf_op jit(solution)/shard_map/attention_backward/pallas_call | solution.py:553
  78.4 2.3 %results.1 = (bf16[512,1024]{1,0:T(8,128)(2,1)}, bf16[512,128]{1,0:T(8,128)(2,1)}, bf16[512,128]{1,0:T(8,128)(2,1)}, bf16[1024,128]{1,0:T(8,128)(2,1)}, bf16[1024,128]{1,0:T(8,128)(2,1)}) custom-call(bf16[512,1024]{1,0:T(8,128)(2,1)} %get-tuple-element.8.out, bf16[512,256]{1,0:T(8,128)(2,1)} %get-tuple-element.9.own, bf16[1024,256]{1,0:T(8,128)(2,1)} %bitcast.3), custom_call_target="tpu_custom_call" | custom-call | tf_op jit(solution)/shard_map/results/pallas_call | solution.py:629

commit v3 on v2

--- a/solution.py
+++ b/solution.py
@@ -8,6 +8,8 @@
 from jax.sharding import PartitionSpec as P
 
 HEAD_DIM = 128
+PER_SOFTEN = 4
+PER_GRADS = 2
 GROUP = 16
 SCALE = HEAD_DIM ** (-0.5)
 LOG2E = 1.4426950408889634
@@ -58,6 +60,7 @@
     score_v,
     dprob_v,
     mask_v,
+    inverse_v,
     grad_v,
     qg_v,
     ownout_v,
@@ -68,7 +71,6 @@
     sib_v,
     hop_v,
     side_v,
-    sum_v,
     in_sem,
     w_sem,
     t_send,
@@ -99,7 +101,7 @@
     y_right, y_left, y_opp = lax.rem(y + 1, ny), lax.rem(y + ny - 1, ny), lax.rem(y + 2, ny)
     right, left, sibling = y_right * 2 + core, y_left * 2 + core, y * 2 + 1 - core
     blocks, block = q_v.shape[0], q_v.shape[1]
-    chunk = send_v.shape[2]
+    chunk = send_v.shape[3]
     width = sib_v.shape[2]
     half = width // 2
     heads = q_v.shape[2] // HEAD_DIM
@@ -127,8 +129,8 @@
 
     def prompt_loads():
         return [
-            pltpu.make_async_copy(src, stage_v.at[:, :, cols], s1_sem.at[what])
-            for what, src, cols in ((0, pk_hbm, key_cols), (1, pv_hbm, value_cols))
+            pltpu.make_async_copy(src, stage_v.at[:, what], s1_sem.at[what])
+            for what, src in enumerate((pk_hbm, pv_hbm))
         ]
 
     for copy in prompt_loads():
@@ -176,11 +178,19 @@
         for dest in range(nmp):
             w_load(dest).start()
 
-    def pick(j):
+    def pick(j, what):
         for g in range(chunk // GROUP):
             rows = pl.ds(g * GROUP, GROUP)
-            picked = dot(choose_v[j], spread_v[:, rows, :].reshape(side, 2 * HEAD_DIM))
-            send_v[j, :, rows, :] = picked.astype(BF16).reshape(n, GROUP, 2 * HEAD_DIM)
+            picked = dot(choose_v[j], spread_v[:, what, rows, :].reshape(side, HEAD_DIM))
+            send_v[j, :, what, rows, :] = picked.astype(BF16).reshape(n, GROUP, HEAD_DIM)
+
+    def hand_out(j, what):
+        to_all(
+            send_v.at[j, :, what], pre_v.at[j, :, what], s2_send.at[j, what], s2_recv.at[j, what]
+        )
+
+    def arrived(ref, sem):
+        pltpu.make_async_copy(ref, ref, sem).wait()
 
     def fetch():
         for peer in peers:
@@ -192,14 +202,14 @@
                 device_id={"dp": peer},
                 device_id_type=MESH,
             ).start()
-        to_all(stage_v, spread_v, s1_send, s1_recv)
+        for what in range(2):
+            to_all(stage_v.at[:, what], spread_v.at[:, what], s1_send.at[what], s1_recv.at[what])
         load_weights()
         row = lax.broadcasted_iota(jnp.int32, (side, side), 0)
         col = lax.broadcasted_iota(jnp.int32, (side, side), 1)
         same = lax.rem(row, GROUP) == lax.rem(col, GROUP)
         prompt_of_col = jnp.where(same, col // GROUP, -1)
-        others = table_v.at[pl.ds(0, n - 1)]
-        pltpu.make_async_copy(others, others, t_recv).wait()
+        arrived(table_v.at[pl.ds(0, n - 1)], t_recv)
 
         for j in range(blocks):
             wanted = jnp.broadcast_to(table_v[:, j : j + 1, :], (n, GROUP, HEAD_DIM))
@@ -210,17 +220,18 @@
                 wanted = wanted[:, :side]
             choose_v[j] = jnp.where(wanted == prompt_of_col, 1.0, 0.0).astype(BF16)
 
-        pltpu.make_async_copy(spread_v, spread_v, s1_recv).wait()
-        for j in range(blocks):
-            pick(j)
-            if j == 0:
-                to_all(send_v.at[j], pre_v.at[j], s2_send.at[j], s2_recv.at[j])
-
-    def part_of(j, t, cols):
+        for what in range(2):
+            arrived(spread_v.at[:, what], s1_recv.at[what])
+            pick(0, what)
+            hand_out(0, what)
+        for j in range(1, blocks):
+            for what in range(2):
+                pick(j, what)
+
+    def part_of(j, t, what):
         if t == tiles:
-            return own_v[j, :, cols]
-        got = pre_v[j, t * per_tile : (t + 1) * per_tile, :, cols]
-        return got.reshape(block, HEAD_DIM)
+            return own_v[j, :, (key_cols, value_cols)[what]]
+        return pre_v[j, t * per_tile : (t + 1) * per_tile, what].reshape(block, HEAD_DIM)
 
     def visible(j):
         place = lax.broadcasted_iota(jnp.int32, (block, block), 1)
@@ -232,74 +243,91 @@
             first = jnp.where(place >= end, end, first)
         return (key >= first) & (key <= place)
 
-    def prepare(j):
+    def wait_keys(j):
         for copy in own_loads(j):
             copy.wait()
-        pltpu.make_async_copy(pre_v.at[j], pre_v.at[j], s2_recv.at[j]).wait()
-        if j + 1 < blocks:
-            to_all(send_v.at[j + 1], pre_v.at[j + 1], s2_send.at[j + 1], s2_recv.at[j + 1])
+        arrived(pre_v.at[j, :, 0], s2_recv.at[j, 0])
+
+    def wait_values(j):
+        arrived(pre_v.at[j, :, 1], s2_recv.at[j, 1])
+
+    def head_cols(h):
+        return pl.ds(pl.multiple_of(h * HEAD_DIM, HEAD_DIM), HEAD_DIM)
+
+    def soften(j):
+        mask_v[...] = jnp.where(visible(j), 0.0, -1e30)
         for t in range(tiles + 1):
-            keys_t[:, t * block : (t + 1) * block] = part_of(j, t, key_cols).T
-        grad_v[...] = jnp.zeros_like(grad_v)
-        mask_v[...] = jnp.where(visible(j), 0.0, -1e30)
-
-    def attend(j, lower, upper):
-        per = 4
-
-        def scores(h, slot):
-            cols = pl.ds(pl.multiple_of(h * HEAD_DIM, HEAD_DIM), HEAD_DIM)
-            qh = q_v[j, :, cols]
+            keys_t[:, t * block : (t + 1) * block] = part_of(j, t, 0).T
+
+        def scores(h):
+            qh = q_v[j, :, head_cols(h)]
             top = None
             for t in range(tiles + 1):
-                s = dot_nt(part_of(j, t, key_cols), qh)
+                s = dot_nt(part_of(j, t, 0), qh)
                 if t == tiles:
                     s = s + mask_v[...]
-                score_v[slot, t] = s
+                score_v[h, t] = s
                 got = fold(s, jnp.max)
                 top = got if top is None else jnp.maximum(top, got)
             return jnp.max(top, axis=0, keepdims=True)
 
-        def middle(h, slot, top):
-            cols = pl.ds(pl.multiple_of(h * HEAD_DIM, HEAD_DIM), HEAD_DIM)
-            doh = do_v[j, :, cols]
+        def powers(h, top):
             total = jnp.zeros((8, block), F32)
+            for t in range(tiles + 1):
+                e = jnp.exp2((score_v[h, t] - top) * (SCALE * LOG2E))
+                score_v[h, t] = e
+                total += fold(e, jnp.sum)
+            inverse = 1.0 / jnp.sum(total, axis=0, keepdims=True)
+            inverse_v[h] = jnp.broadcast_to(inverse, (8, block))
+
+        per = PER_SOFTEN
+
+        def step(i, carry):
+            hs = [i * per + s for s in range(per)]
+            tops = [scores(h) for h in hs]
+            for h, top in zip(hs, tops):
+                powers(h, top)
+            return carry
+
+        lax.fori_loop(0, heads // per, step, 0)
+
+    def attend(j, lower, upper):
+        def middle(h, slot):
+            doh = do_v[j, :, head_cols(h)]
             mixed = jnp.zeros((8, block), F32)
             for t in range(tiles + 1):
-                dp = dot_nt(part_of(j, t, value_cols), doh)
+                dp = dot_nt(part_of(j, t, 1), doh)
                 dprob_v[slot, t] = dp
-                e = jnp.exp2((score_v[slot, t] - top) * (SCALE * LOG2E))
-                score_v[slot, t] = e
-                total += fold(e, jnp.sum)
-                mixed += fold(e * dp, jnp.sum)
-            inverse = 1.0 / jnp.sum(total, axis=0, keepdims=True)
-            delta = jnp.sum(mixed, axis=0, keepdims=True) * inverse
-            return inverse, delta
+                mixed += fold(score_v[h, t] * dp, jnp.sum)
+            inverse = inverse_v[h, 0:1, :]
+            return inverse, jnp.sum(mixed, axis=0, keepdims=True) * inverse
 
         def grads(hs, stats):
-            colss = [pl.ds(pl.multiple_of(h * HEAD_DIM, HEAD_DIM), HEAD_DIM) for h in hs]
-            qs = jnp.concatenate([q_v[j, :, c] for c in colss], axis=0)
-            dos = jnp.concatenate([do_v[j, :, c] for c in colss], axis=0)
+            qs = jnp.concatenate([q_v[j, :, head_cols(h)] for h in hs], axis=0)
+            dos = jnp.concatenate([do_v[j, :, head_cols(h)] for h in hs], axis=0)
             dqs = [jnp.zeros((HEAD_DIM, block), F32) for _ in hs]
             for t in range(tiles + 1):
                 dss, ps = [], []
                 for slot, (inverse, delta) in enumerate(stats):
-                    prob = score_v[slot, t] * inverse
+                    prob = score_v[hs[slot], t] * inverse
                     ds = (prob * (dprob_v[slot, t] - delta)).astype(BF16)
                     dss.append(ds)
                     ps.append(prob.astype(BF16))
                     dqs[slot] += dot(keys_t[:, t * block : (t + 1) * block], ds)
                 grad_v[t, :, key_cols] += dot(jnp.concatenate(dss, axis=1), qs)
                 grad_v[t, :, value_cols] += dot(jnp.concatenate(ps, axis=1), dos)
-            for c, dq in zip(colss, dqs):
-                qg_v[j, c, :] = (dq * SCALE).astype(BF16)
+            for h, dq in zip(hs, dqs):
+                qg_v[j, head_cols(h), :] = (dq * SCALE).astype(BF16)
+
+        per = PER_GRADS
 
         def step(i, carry):
             hs = [i * per + s for s in range(per)]
-            tops = [scores(h, s) for s, h in enumerate(hs)]
-            stats = [middle(h, s, top) for s, (h, top) in enumerate(zip(hs, tops))]
-            grads(hs, stats)
+            grads(hs, [middle(h, s) for s, h in enumerate(hs)])
             return carry
 
+        if lower == 0:
+            grad_v[...] = jnp.zeros_like(grad_v)
         lax.fori_loop(lower // per, upper // per, step, 0)
 
     def rounded(t):
@@ -332,10 +360,10 @@
 
         to_all(home_v, pre_hbm, h_send, h_recv)
 
-    def project(j, dest):
-        if j == 0:
+    def project(j, dest, first=0, last=2):
+        if j == 0 and first == 0:
             w_load(dest).wait()
-        step = min(512, width)
+        step = width // 2
 
         def tile(i, carry):
             rows = pl.ds(pl.multiple_of(i * step, step), step)
@@ -343,7 +371,7 @@
             part_v[j, dest, rows, :] = dot(w_v[from_w, :], qg_v[j]).astype(BF16)
             return carry
 
-        lax.fori_loop(0, width // step, tile, 0)
+        lax.fori_loop(first, last, tile, 0)
 
     def to_sibling(j, y_dest, slot):
         return pltpu.make_async_remote_copy(
@@ -402,6 +430,7 @@
         for p in range(pieces):
             for way in range(2):
                 opposite(j, way, p).start()
+        give_back(j)
         project(j, y_left * 2 + 1 - core)
         to_sibling(j, y_left, 2).start()
         project(j, y_right * 2 + core)
@@ -430,7 +459,7 @@
         cols = piece_rows(way, p)
         rows = pl.ds(j * block, block)
         return pltpu.make_async_copy(
-            sum_v.at[j, :, cols], out_hbm.at[rows, cols], out_sem.at[j, 1 + way * pieces + p]
+            q_v.at[j, :, cols], out_hbm.at[rows, cols], out_sem.at[j, 1 + way * pieces + p]
         )
 
     def finish(j):
@@ -445,7 +474,7 @@
                 added += side_v[j, 1 - way, rows, :].astype(F32)
                 mixed(j, way, p).wait_recv()
                 added += side_v[j, way, rows, :].astype(F32)
-                sum_v[j, :, rows] = added.astype(BF16).T
+                q_v[j, :, rows] = added.astype(BF16).T
                 out_copy(j, way, p).start()
 
     def all_but_one(ref, sem):
@@ -454,9 +483,10 @@
 
     def end_fetch():
         all_but_one(table_v, t_send)
-        all_but_one(spread_v, s1_send)
-        for j in range(blocks):
-            all_but_one(send_v.at[j], s2_send.at[j])
+        for what in range(2):
+            all_but_one(spread_v.at[:, what], s1_send.at[what])
+            for j in range(blocks):
+                all_but_one(send_v.at[j, :, what], s2_send.at[j, what])
 
     def end_back():
         all_but_one(home_v, h_send)
@@ -478,21 +508,24 @@
                 out_copy(j, way, p).wait()
 
     fetch()
-    prepare(0)
+    wait_keys(0)
+    soften(0)
+    wait_values(0)
+    for what in range(2):
+        hand_out(1, what)
     attend(0, 0, heads)
-    give_back(0)
     send_partials(0)
-    prepare(1)
-    attend(1, 0, heads // 2)
+    wait_keys(1)
+    wait_values(1)
+    soften(1)
     pass_on(0, 0)
     pass_on(0, 1)
-    attend(1, heads // 2, heads)
-    give_back(1)
+    attend(1, 0, heads)
     send_partials(1)
+    pass_on(1, 0)
     finish(0)
+    pass_on(1, 1)
     bring_home()
-    pass_on(1, 0)
-    pass_on(1, 1)
     finish(1)
     end_fetch()
     end_back()
@@ -565,15 +598,16 @@
             pltpu.VMEM((blocks, block, two), BF16),
             pltpu.VMEM(q_weight.shape, BF16),
             pltpu.VMEM((n, blocks, HEAD_DIM), jnp.int32),
-            pltpu.VMEM((n, chunk, two), BF16),
-            pltpu.VMEM((n, chunk, two), BF16),
+            pltpu.VMEM((n, 2, chunk, HEAD_DIM), BF16),
+            pltpu.VMEM((n, 2, chunk, HEAD_DIM), BF16),
             pltpu.VMEM((blocks, n * GROUP, n * GROUP), BF16),
-            pltpu.VMEM((blocks, n, chunk, two), BF16),
-            pltpu.VMEM((blocks, n, chunk, two), BF16),
+            pltpu.VMEM((blocks, n, 2, chunk, HEAD_DIM), BF16),
+            pltpu.VMEM((blocks, n, 2, chunk, HEAD_DIM), BF16),
             pltpu.VMEM((HEAD_DIM, prefix + block), BF16),
-            pltpu.VMEM((4, tiles + 1, block, block), F32),
-            pltpu.VMEM((4, tiles + 1, block, block), F32),
+            pltpu.VMEM((cols // HEAD_DIM, tiles + 1, block, block), F32),
+            pltpu.VMEM((PER_GRADS, tiles + 1, block, block), F32),
             pltpu.VMEM((block, block), F32),
+            pltpu.VMEM((cols // HEAD_DIM, 8, block), F32),
             pltpu.VMEM((tiles + 1, block, two), F32),
             pltpu.VMEM((blocks, cols, block), BF16),
             pltpu.VMEM((blocks, block, two), BF16),
@@ -584,16 +618,15 @@
             pltpu.VMEM((blocks, nmp // 2, width, block), BF16),
             pltpu.VMEM((blocks, 2, width // 2, block), BF16),
             pltpu.VMEM((blocks, 2, width, block), BF16),
-            pltpu.VMEM((blocks, block, width), BF16),
             dma((blocks, 4)),
             dma((nmp,)),
             dma,
             dma,
             dma((2,)),
-            dma,
-            dma,
-            dma((blocks,)),
-            dma((blocks,)),
+            dma((2,)),
+            dma((2,)),
+            dma((blocks, 2)),
+            dma((blocks, 2)),
             dma((blocks,)),
             dma((blocks,)),
             dma,

time: 81.1 us -> 79.8 us (0.984)
  Pallas kernels: 80.1 us -> 78.8 us
    pallas_call x1, Pallas kernels: 77.8 us -> 76.4 us  [shards(): pl.pallas_call(functools.partial(kernel, n, nmp), out_shape=(jax.ShapeDty...]
where the time goes in v3:
time: 79.8 us; the launch traced here: 79.6 us
  Pallas kernels  78.8 us (99%)
  between operations  0.8 us (1%)
    pallas_call x1, Pallas kernels, shards(): pl.pallas_call(functools.partial(kernel, n, nmp), out_shape=(jax.ShapeDty...  76.4 us
    pallas_call x1, Pallas kernels, shards(): pl.pallas_call(results, out_shape=(jax.ShapeDtypeStruct((rows, width), BF...  2.35 us

profile of v3, /device:TPU:1, one launch (start us, length us, event | category | flops | bytes accessed | tf_op | source)
XLA Modules:
  0.0 79.6 jit_solution(1398073217179156591)
XLA Ops:
  0.6 76.4 %attention_backward.1 = (bf16[512,1024]{1,0:T(8,128)(2,1)}, bf16[512,256]{1,0:T(8,128)(2,1)}, bf16[16,64,256]{2,1,0:T(8,128)(2,1)}) custom-call(s32[2]{0:T(128)} %prompt_ref.1, s32[2,4]{1,0:T(2,128)} %lengths_ref.1, bf16[512,1024]{1,0:T(8,128)(2,1)} %q_hbm.1, bf16[512,1024]{1,0:T(8,128)(2,1)} %do_hbm.1, bf16[512,128]{1,0:T(8,128)(2,1)} %rk_hbm.1, ...), custom_call_target="tpu_custom_call" | custom-call | flops 15300820992 | bytes 16777216 | tf_op jit(solution)/shard_map/attention_backward/pallas_call | solution.py:586
  77.1 2.3 %results.1 = (bf16[512,1024]{1,0:T(8,128)(2,1)}, bf16[512,128]{1,0:T(8,128)(2,1)}, bf16[512,128]{1,0:T(8,128)(2,1)}, bf16[1024,128]{1,0:T(8,128)(2,1)}, bf16[1024,128]{1,0:T(8,128)(2,1)}) custom-call(bf16[512,1024]{1,0:T(8,128)(2,1)} %get-tuple-element.8.out, bf16[512,256]{1,0:T(8,128)(2,1)} %get-tuple-element.9.own, bf16[1024,256]{1,0:T(8,128)(2,1)} %bitcast.3), custom_call_target="tpu_custom_call" | custom-call | tf_op jit(solution)/shard_map/results/pallas_call | solution.py:662

commit v4 on v3

--- a/solution.py
+++ b/solution.py
@@ -9,7 +9,7 @@
 
 HEAD_DIM = 128
 PER_SOFTEN = 4
-PER_GRADS = 2
+PER_GRADS = 4
 GROUP = 16
 SCALE = HEAD_DIM ** (-0.5)
 LOG2E = 1.4426950408889634
@@ -184,10 +184,12 @@
             picked = dot(choose_v[j], spread_v[:, what, rows, :].reshape(side, HEAD_DIM))
             send_v[j, :, what, rows, :] = picked.astype(BF16).reshape(n, GROUP, HEAD_DIM)
 
-    def hand_out(j, what):
-        to_all(
-            send_v.at[j, :, what], pre_v.at[j, :, what], s2_send.at[j, what], s2_recv.at[j, what]
-        )
+    def hand_out(j, what=None):
+        if what is None:
+            to_all(send_v.at[j], pre_v.at[j], s2_send.at[j, 0], s2_recv.at[j, 0])
+        else:
+            sems = s2_send.at[j, what], s2_recv.at[j, what]
+            to_all(send_v.at[j, :, what], pre_v.at[j, :, what], *sems)
 
     def arrived(ref, sem):
         pltpu.make_async_copy(ref, ref, sem).wait()
@@ -246,7 +248,7 @@
     def wait_keys(j):
         for copy in own_loads(j):
             copy.wait()
-        arrived(pre_v.at[j, :, 0], s2_recv.at[j, 0])
+        arrived(pre_v.at[j, :, 0] if j == 0 else pre_v.at[j], s2_recv.at[j, 0])
 
     def wait_values(j):
         arrived(pre_v.at[j, :, 1], s2_recv.at[j, 1])
@@ -485,8 +487,9 @@
         all_but_one(table_v, t_send)
         for what in range(2):
             all_but_one(spread_v.at[:, what], s1_send.at[what])
-            for j in range(blocks):
-                all_but_one(send_v.at[j, :, what], s2_send.at[j, what])
+            all_but_one(send_v.at[0, :, what], s2_send.at[0, what])
+        for j in range(1, blocks):
+            all_but_one(send_v.at[j], s2_send.at[j, 0])
 
     def end_back():
         all_but_one(home_v, h_send)
@@ -511,12 +514,10 @@
     wait_keys(0)
     soften(0)
     wait_values(0)
-    for what in range(2):
-        hand_out(1, what)
+    hand_out(1)
     attend(0, 0, heads)
     send_partials(0)
     wait_keys(1)
-    wait_values(1)
     soften(1)
     pass_on(0, 0)
     pass_on(0, 1)
@@ -642,7 +643,7 @@
             dma((blocks, 5)),
         ],
         compiler_params=pltpu.CompilerParams(
-            collective_id=0, has_side_effects=True, vmem_limit_bytes=60 * 2**20
+            collective_id=0, has_side_effects=True, vmem_limit_bytes=63 * 2**20
         ),
         cost_estimate=pl.CostEstimate(
             flops=flops, bytes_accessed=2 * q_weight.size, transcendentals=0

time: 79.8 us -> 78.7 us (0.986)
  Pallas kernels: 78.8 us -> 77.7 us
    pallas_call x1, Pallas kernels: 76.4 us -> 75.3 us  [shards(): pl.pallas_call(functools.partial(kernel, n, nmp), out_shape=(jax.ShapeDty...]
where the time goes in v4:
time: 78.7 us; the launch traced here: 78.5 us
  Pallas kernels  77.7 us (99%)
  between operations  0.8 us (1%)
    pallas_call x1, Pallas kernels, shards(): pl.pallas_call(functools.partial(kernel, n, nmp), out_shape=(jax.ShapeDty...  75.3 us
    pallas_call x1, Pallas kernels, shards(): pl.pallas_call(results, out_shape=(jax.ShapeDtypeStruct((rows, width), BF...  2.35 us

profile of v4, /device:TPU:1, one launch (start us, length us, event | category | flops | bytes accessed | tf_op | source)
XLA Modules:
  0.0 78.5 jit_solution(14544257296973794438)
XLA Ops:
  0.6 75.3 %attention_backward.1 = (bf16[512,1024]{1,0:T(8,128)(2,1)}, bf16[512,256]{1,0:T(8,128)(2,1)}, bf16[16,64,256]{2,1,0:T(8,128)(2,1)}) custom-call(s32[2]{0:T(128)} %prompt_ref.1, s32[2,4]{1,0:T(2,128)} %lengths_ref.1, bf16[512,1024]{1,0:T(8,128)(2,1)} %q_hbm.1, bf16[512,1024]{1,0:T(8,128)(2,1)} %do_hbm.1, bf16[512,128]{1,0:T(8,128)(2,1)} %rk_hbm.1, ...), custom_call_target="tpu_custom_call" | custom-call | flops 15300820992 | bytes 16777216 | tf_op jit(solution)/shard_map/attention_backward/pallas_call | solution.py:587
  76.0 2.3 %results.1 = (bf16[512,1024]{1,0:T(8,128)(2,1)}, bf16[512,128]{1,0:T(8,128)(2,1)}, bf16[512,128]{1,0:T(8,128)(2,1)}, bf16[1024,128]{1,0:T(8,128)(2,1)}, bf16[1024,128]{1,0:T(8,128)(2,1)}) custom-call(bf16[512,1024]{1,0:T(8,128)(2,1)} %get-tuple-element.8.out, bf16[512,256]{1,0:T(8,128)(2,1)} %get-tuple-element.9.own, bf16[1024,256]{1,0:T(8,128)(2,1)} %bitcast.3), custom_call_target="tpu_custom_call" | custom-call | tf_op jit(solution)/shard_map/results/pallas_call | solution.py:663
